TPU v7x, 128 devices: a whole 4x4x4 slice. The times are simulated.
128 devices in a mesh: slab: 16 (over z, x), helper: 8 (over y, core).
Axes of the slice: x: 4, y: 4, z: 4, core: 2. Of those that a mesh axis runs over, the one named last changes fastest.
Arguments:
- disp: float32 [400, 3, 16384], P(None, None, ('slab', 'helper')), may hold values from -2 to 2
- strain: float32 [9, 16384], P(None, ('slab', 'helper')), may hold values from -6 to 6
- counts: int32 [16384], P(('slab', 'helper')), may hold values from 3 to 12
- assign: int32 [16384, 1], P(('slab', 'helper')), may hold values from 0 to 127; in each aligned block of 128 rows (0 to 127, 128 to 255, ...) at most 2 rows name the same one
- cached_pos: float32 [400, 3, 32768], P(None, None, ('slab', 'helper')), may hold values from -1 to 1
- contact_mask: int32 [400, 400], replicated, may hold values from 0 to 1, as said below
- node_index: int32 [8, 16384], P(None, ('slab', 'helper')), may hold values from 0 to 4095, as said below
- node_grads: float32 [3, 8, 16384], P(None, None, ('slab', 'helper')), may hold values from -6 to 6
Outputs:
- disp_out: float32 [400, 3, 16384], P(None, None, ('slab', 'helper'))
- stress: float32 [9, 16384], P(None, ('slab', 'helper'))
- grid_force: float32 [3, 32, 1024], P(None, 'slab', 'helper')
Inputs may be any that keep to these rules, and one draw needn't show every extreme that they name: `contact_mask`: symmetric 0/1 matrix with zero diagonal. `node_index`: each point's eight values are the corners of one cell: layers l and l + 1 with l from 0 to 2, rows i and i + 1, columns j and j + 1 of a 32 x 32 layer, value layer * 1024 + row * 32 + column. `assign`: within one device's 128 points no helper is named more than 2 times. `cached_pos`: column d * 128 * 2 + s * 2 + c holds the packing of the c-th point, in order, among the points of block s that name helper d; other columns are not used.
All inputs are finite; a program needn't handle non-finite values.
Results may differ from a plain program's by a relative error of at most 0.0003.
Values sent between devices are 32-bit elements; how exact they have to be, the bound alone decides.
A program may use at most 64 MiB of HBM per device.

v0:
```python
import jax
import jax.numpy as jnp
from jax import lax
from jax.sharding import PartitionSpec as P

IT_HI = 12
LAYERS = 2
PLANE = 1024


OMEGA = 0.8
GROUND = 1.0
HIGHEST = lax.Precision.HIGHEST


def shifted(x, axis, by):
    length = lax.axis_size(axis)
    pairs = [(i, i + by) for i in range(length) if 0 <= i + by < length]
    return lax.ppermute(x, axis, pairs)


def relax(start, loading, sweeps_of, stiff, scale):
    grains = start.shape[0]

    def sweep(sweep_index, current):
        mixed = jnp.dot(stiff, current.reshape(grains, -1), precision=HIGHEST).reshape(
            current.shape
        )
        updated = current + OMEGA * (loading - scale * current + mixed) / scale
        return jnp.where(sweep_index < sweeps_of, updated, current)

    trips = IT_HI
    return lax.fori_loop(0, trips, sweep, start)


def packing_stress(relaxed, pos, stiff, scale):
    grains = relaxed.shape[0]
    mixed = jnp.dot(stiff, relaxed.reshape(grains, -1), precision=HIGHEST).reshape(relaxed.shape)
    internal = scale * relaxed - mixed
    moments = jnp.einsum("gdp,gep->dep", internal, pos, precision=HIGHEST) / grains
    return 0.5 * (moments + jnp.transpose(moments, (1, 0, 2)))


def solve_points(start, strain_cols, pos, sweeps_of, stiff, scale):
    strain_mat = strain_cols.reshape(3, 3, -1)
    loading = jnp.einsum("dep,gep->gdp", strain_mat, pos, precision=HIGHEST)
    relaxed = relax(start, loading, sweeps_of, stiff, scale)
    return (relaxed, packing_stress(relaxed, pos, stiff, scale))


def neighbor(rim_layer, offset):
    return shifted(rim_layer, "slab", offset)


def per_device(disp, strain, counts, assign, cached_pos, contact_mask, node_index, node_grads):
    grains = disp.shape[0]
    points = disp.shape[2]
    devices = lax.axis_size(("slab", "helper"))
    capacity = cached_pos.shape[2] // devices
    stiff = contact_mask.astype(jnp.float32)
    scale = (jnp.sum(stiff, axis=1) + GROUND)[:, None, None]
    target = assign[:, 0]
    order = jnp.arange(points, dtype=jnp.int32)
    same = target[:, None] == target[None, :]
    earlier = order[None, :] < order[:, None]
    position = jnp.sum((same & earlier).astype(jnp.int32), axis=1)
    column = target * capacity + position
    slots = devices * capacity
    owner_of = column[None, :] == jnp.arange(slots, dtype=jnp.int32)[:, None]
    filled = jnp.any(owner_of, axis=1)
    chosen = jnp.sum(jnp.where(owner_of, order[None, :], 0), axis=1)
    send_disp = jnp.take(disp, chosen, axis=2).reshape(grains, 3, devices, capacity)
    send_strain = jnp.take(strain, chosen, axis=1).reshape(9, 1, devices, capacity)
    send_counts = (
        jnp.where(filled, jnp.take(counts, chosen), 0)
        .astype(jnp.float32)
        .reshape(1, 1, devices, capacity)
    )
    got_disp, got_strain, got_counts = (
        lax.all_to_all(send_disp, ("slab", "helper"), split_axis=2, concat_axis=2, tiled=True),
        lax.all_to_all(send_strain, ("slab", "helper"), split_axis=2, concat_axis=2, tiled=True),
        lax.all_to_all(send_counts, ("slab", "helper"), split_axis=2, concat_axis=2, tiled=True),
    )
    sweeps_of = got_counts.reshape(-1).astype(jnp.int32)
    relaxed, sigma = solve_points(
        got_disp.reshape(grains, 3, slots),
        got_strain.reshape(9, slots),
        cached_pos,
        sweeps_of,
        stiff,
        scale,
    )
    back_disp, back_sigma = (
        lax.all_to_all(
            relaxed.reshape(grains, 3, devices, capacity),
            ("slab", "helper"),
            split_axis=2,
            concat_axis=2,
            tiled=True,
        ),
        lax.all_to_all(
            sigma.reshape(9, 1, devices, capacity),
            ("slab", "helper"),
            split_axis=2,
            concat_axis=2,
            tiled=True,
        ),
    )
    disp_out = jnp.take(back_disp.reshape(grains, 3, slots), column, axis=2)
    stress = jnp.take(back_sigma.reshape(9, slots), column, axis=1)
    sigma_mat = stress.reshape(3, 3, points)
    contrib = jnp.einsum("cdp,dkp->ckp", -sigma_mat, node_grads, precision=HIGHEST)
    extended = (
        jnp.zeros((3, (LAYERS + 2) * PLANE), jnp.float32)
        .at[:, node_index.reshape(-1)]
        .add(contrib.reshape(3, -1))
    )
    shared = lax.psum_scatter(
        extended.reshape(3, LAYERS + 2, PLANE), "helper", scatter_dimension=2, tiled=True
    )
    from_below = neighbor(shared[:, LAYERS + 1], 1)
    from_above = neighbor(shared[:, 0], -1)
    grid_force = shared[:, 1 : LAYERS + 1]
    grid_force = grid_force.at[:, 0].add(from_below)
    grid_force = grid_force.at[:, LAYERS - 1].add(from_above)
    return (disp_out, stress, grid_force)


def solution(mesh):
    placed = (
        P(None, None, ("slab", "helper")),
        P(None, ("slab", "helper")),
        P(("slab", "helper")),
        P(("slab", "helper"), None),
        P(None, None, ("slab", "helper")),
        P(),
        P(None, ("slab", "helper")),
        P(None, None, ("slab", "helper")),
    )
    return jax.shard_map(
        per_device,
        mesh=mesh,
        in_specs=placed,
        out_specs=(
            P(None, None, ("slab", "helper")),
            P(None, ("slab", "helper")),
            P(None, "slab", "helper"),
        ),
        check_vma=False,
    )
```

profile of v0, /device:TPU:6, one launch (start us, length us, event | category | flops | bytes accessed | tf_op | source)
XLA Modules:
  0.0 250.5 jit_solution(10497043931404213202)
XLA Ops:
  12.4 10.5 %all-to-all-start.1 = ((f32[1,1,128,2]{3,1,0,2:T(1,128)}), f32[1,1,128,2]{3,1,0,2:T(1,128)S(1)}, u32[]{:S(2)}, u32[]{:S(2)}) async-start(f32[1,1,128,2]{3,1,0,2:T(1,128)} %copy.164), calls=%async_computation.1 | async-start | bytes 131072 | tf_op jit(solution)/shard_map/all_to_all | solution.py:82
  27.1 4.0 %all-to-all-done.1 = f32[1,1,128,2]{3,1,0,2:T(1,128)S(1)} async-done(((f32[1,1,128,2]{3,1,0,2:T(1,128)}), f32[1,1,128,2]{3,1,0,2:T(1,128)S(1)}, u32[]{:S(2)}, u32[]{:S(2)}) %all-to-all-start.1) | async-done | bytes 1056 | tf_op jit(solution)/shard_map/all_to_all | solution.py:82
  31.1 5.8 %all-to-all-start.2 = ((f32[9,1,128,2]{0,3,1,2:T(2,128)}), f32[9,1,128,2]{0,3,1,2:T(2,128)S(1)}, u32[]{:S(2)}, u32[]{:S(2)}) async-start(f32[9,1,128,2]{0,3,1,2:T(2,128)} %broadcast_select_fusion), calls=%async_computation.2 | async-start | bytes 262144 | tf_op jit(solution)/shard_map/all_to_all | solution.py:81
  39.0 3.1 %copy.157 = f32[400,3,128,2]{0,3,1,2:T(2,128)} copy(f32[400,3,128,2]{0,3,2,1:T(2,128)} %copy_select_fusion) | data formatting | bytes 2457600 | tf_op jit(solution)/shard_map/jit(_take)/select_n | solution.py:72
  45.3 10.2 %all-to-all-start = ((f32[400,3,128,2]{0,3,1,2:T(2,128)}), f32[400,3,128,2]{0,3,1,2:T(2,128)}, u32[]{:S(2)}, u32[]{:S(2)}) async-start(f32[400,3,128,2]{0,3,1,2:T(2,128)} %copy.157), calls=%async_computation | async-start | bytes 3145728 | tf_op jit(solution)/shard_map/all_to_all | solution.py:80
  56.3 4.8 %convolution_bitcast_fusion = f32[400,3,256]{0,1,2:T(4,128)} fusion(f32[3,3,256]{1,0,2:T(4,128)S(1)} %reshape.333, f32[400,3,256]{0,1,2:T(4,128)S(1)} %copy.169), kind=kOutput, calls=%fused_computation.15 | convolution fusion | flops 11059200 | bytes 2466816 | tf_op jit(solution)/shard_map/dep,gep->gdp/dot_general | solution.py:46
  61.1 2.7 %copy.171 = f32[400,3,256]{2,0,1:T(8,128)} copy(f32[400,3,256]{0,1,2:T(4,128)} %convolution_bitcast_fusion) | data formatting | bytes 2457600 | tf_op jit(solution)/shard_map/while | solution.py:33
  63.8 15.0 %all-to-all-done = f32[400,3,128,2]{0,3,1,2:T(2,128)} async-done(((f32[400,3,128,2]{0,3,1,2:T(2,128)}), f32[400,3,128,2]{0,3,1,2:T(2,128)}, u32[]{:S(2)}, u32[]{:S(2)}) %all-to-all-start) | async-done | bytes 1228832 | tf_op jit(solution)/shard_map/all_to_all | solution.py:80
  78.9 3.1 %copy.158 = f32[400,3,128,2]{0,3,2,1:T(2,128)} copy(f32[400,3,128,2]{0,3,1,2:T(2,128)} %all-to-all-done) | data formatting | bytes 2457600 | tf_op jit(solution)/shard_map/all_to_all | solution.py:80
  82.0 3.2 %reshape.272 = f32[400,3,256]{0,2,1:T(8,128)} reshape(f32[400,3,128,2]{0,3,2,1:T(2,128)} %copy.158) | data formatting | bytes 2457600 | tf_op jit(solution)/shard_map/reshape | solution.py:86
  87.0 47.7 %while.15 = (s32[]{:T(128)}, f32[400,3,256]{2,0,1:T(8,128)S(1)}, s32[256]{0:T(256)S(1)}, f32[400,1,1]{0,2,1:T(1,128)S(1)}, f32[400,3,256]{2,0,1:T(8,128)}, /*index=5*/f32[400,400]{1,0:T(8,128)}, s32[]{:T(128)}) while((s32[]{:T(128)}, f32[400,3,256]{2,0,1:T(8,128)S(1)}, s32[256]{0:T(256)S(1)}, f32[400,1,1]{0,2,1:T(1,128)S(1)}, ...), condition=%wide.region_5.6_spmd, body=%wide.region_4.5_spmd.sunk | while | flops 1476710656 | bytes 14262481 | solution.py:33
  88.5 2.4 add_select_fusion.2
  92.5 2.4 add_select_fusion.2
  96.5 2.4 add_select_fusion.2
  139.3 2.9 %copy.178 = f32[400,3,256]{0,1,2:T(4,128)} copy(f32[400,3,256]{2,0,1:T(8,128)} %bitcast_subtract_fusion) | data formatting | bytes 2457600 | tf_op jit(solution)/shard_map/sub | solution.py:39
  142.2 10.4 %fusion.17 = f32[256,3,3]{2,1,0:T(4,128)} fusion(f32[400,3,256]{0,1,2:T(4,128)} %copy.178, f32[400,3,256]{0,1,2:T(4,128)S(1)} %copy.169), kind=kOutput, calls=%fused_computation.60 | convolution fusion | flops 11059200 | bytes 2466816 | tf_op jit(solution)/shard_map/gdp,gep->dep/dot_general | solution.py:40
  156.0 5.5 %all-to-all-start.4 = ((f32[9,1,128,2]{0,3,1,2:T(2,128)}), f32[9,1,128,2]{0,3,1,2:T(2,128)S(1)}, u32[]{:S(2)}, u32[]{:S(2)}) async-start(f32[9,1,128,2]{0,3,1,2:T(2,128)} %copy.182), calls=%async_computation.4 | async-start | bytes 262144 | tf_op jit(solution)/shard_map/all_to_all | solution.py:101
  167.3 2.7 %all-to-all-done.4 = f32[9,1,128,2]{0,3,1,2:T(2,128)S(1)} async-done(((f32[9,1,128,2]{0,3,1,2:T(2,128)}), f32[9,1,128,2]{0,3,1,2:T(2,128)S(1)}, u32[]{:S(2)}, u32[]{:S(2)}) %all-to-all-start.4) | async-done | bytes 9248 | tf_op jit(solution)/shard_map/all_to_all | solution.py:101
  170.0 7.6 %all-to-all-start.3 = ((f32[400,3,128,2]{0,3,1,2:T(2,128)}), f32[400,3,128,2]{0,3,1,2:T(2,128)}, u32[]{:S(2)}, u32[]{:S(2)}) async-start(f32[400,3,128,2]{0,3,1,2:T(2,128)} %copy.173), calls=%async_computation.3 | async-start | bytes 3145728 | tf_op jit(solution)/shard_map/all_to_all | solution.py:94
  179.9 7.7 %scatter_custom_fusion = f32[3,4096]{0,1:T(8,128)} fusion(s32[1024]{0:T(1024)S(1)} %bitcast.128, f32[1024,3]{1,0:T(8,128)S(1)} %copy.187, f32[]{:T(128)} %constant.147.clone.1), kind=kCustom, calls=%fused_computation.20 | custom fusion | flops 3072 | bytes 49156 | tf_op jit(solution)/shard_map/scatter-add | solution.py:116
  187.6 2.9 %copy.220 = f32[3,4,1024]{0,1,2:T(4,128)S(1)} copy(f32[3,4,1024]{0,2,1:T(8,128)} %bitcast.110) | data formatting | bytes 98304
  192.3 32.7 %reduce-scatter.4.cloned.1.call-done = f32[128,12]{1,0:T(8,128)} async-done(((f32[1024,12]{1,0:T(8,128)}), f32[128,12]{1,0:T(8,128)}) %reduce-scatter.4.cloned.1.call-update) | async-done | bytes 6160
  226.1 3.5 %collective-permute-start = (f32[3,128]{1,0:T(4,128)S(1)}, f32[3,128]{1,0:T(4,128)S(1)}, u32[]{:S(2)}, u32[]{:S(2)}) collective-permute-start(f32[3,128]{1,0:T(4,128)S(1)} %bitcast.129), channel_id=1, source_target_pairs={{0,8},{8,16},{16,24},{24,32},{32,40},{40,48},{48,56},{56,64},{64,7... | collective-permute-start | bytes 4616 | tf_op jit(solution)/shard_map/ppermute | solution.py:19
  233.1 5.2 %collective-permute-done.1 = f32[3,128]{1,0:T(4,128)S(1)} collective-permute-done((f32[3,128]{1,0:T(4,128)S(1)}, f32[3,128]{1,0:T(4,128)S(1)}, u32[]{:S(2)}, u32[]{:S(2)}) %collective-permute-start.1) | collective-permute-done | bytes 1568 | tf_op jit(solution)/shard_map/ppermute | solution.py:19
  (175 shorter events, 84.5 us)
Async XLA Ops:
  7.2 2.3 copy-start
  7.2 15.8 %copy-start.7 = (f32[9,128]{1,0:T(8,128)S(1)}, f32[9,128]{1,0:T(8,128)}, u32[]{:S(2)}) copy-start(f32[9,128]{1,0:T(8,128)} %param.15) | copy-start | bytes 13828
  7.2 17.5 %copy-start.5 = (f32[400,3,128]{2,0,1:T(8,128)S(1)}, f32[400,3,128]{2,0,1:T(8,128)}, u32[]{:S(2)}) copy-start(f32[400,3,128]{2,0,1:T(8,128)} %param.14) | copy-start | bytes 1843204
  12.4 18.7 %all-to-all-start.1 = ((f32[1,1,128,2]{3,1,0,2:T(1,128)}), f32[1,1,128,2]{3,1,0,2:T(1,128)S(1)}, u32[]{:S(2)}, u32[]{:S(2)}) async-start(f32[1,1,128,2]{3,1,0,2:T(1,128)} %copy.164), calls=%async_computation.1 | async-start | bytes 131072 | tf_op jit(solution)/shard_map/all_to_all | solution.py:82
  31.1 14.1 %all-to-all-start.2 = ((f32[9,1,128,2]{0,3,1,2:T(2,128)}), f32[9,1,128,2]{0,3,1,2:T(2,128)S(1)}, u32[]{:S(2)}, u32[]{:S(2)}) async-start(f32[9,1,128,2]{0,3,1,2:T(2,128)} %broadcast_select_fusion), calls=%async_computation.2 | async-start | bytes 262144 | tf_op jit(solution)/shard_map/all_to_all | solution.py:81
  42.1 2.2 copy-start.1
  45.2 10.3 %copy-start.9 = (s32[128,1]{0,1:T(1,128)S(1)}, s32[128,1]{0,1:T(1,128)}, u32[]{:S(2)}) copy-start(s32[128,1]{0,1:T(1,128)} %param.17) | copy-start | bytes 1540
  45.2 10.4 %copy-start.8 = (s32[8,128]{1,0:T(8,128)S(1)}, s32[8,128]{1,0:T(8,128)}, u32[]{:S(2)}) copy-start(s32[8,128]{1,0:T(8,128)} %param.20) | copy-start | bytes 12292
  45.3 33.6 %all-to-all-start = ((f32[400,3,128,2]{0,3,1,2:T(2,128)}), f32[400,3,128,2]{0,3,1,2:T(2,128)}, u32[]{:S(2)}, u32[]{:S(2)}) async-start(f32[400,3,128,2]{0,3,1,2:T(2,128)} %copy.157), calls=%async_computation | async-start | bytes 3145728 | tf_op jit(solution)/shard_map/all_to_all | solution.py:80
  87.0 1.5 copy-start.4
  91.0 1.5 copy-start.4
  95.0 1.5 copy-start.4
  99.0 1.5 copy-start.4
  102.9 1.5 copy-start.4
  106.9 1.5 copy-start.4
  110.9 1.5 copy-start.4
  114.9 1.5 copy-start.4
  130.8 1.5 copy-start.4
  152.7 8.9 %copy-start.6 = (f32[3,8,128]{2,1,0:T(8,128)S(1)}, f32[3,8,128]{2,1,0:T(8,128)}, u32[]{:S(2)}) copy-start(f32[3,8,128]{2,1,0:T(8,128)} %param.21) | copy-start | bytes 36868
  156.0 14.0 %all-to-all-start.4 = ((f32[9,1,128,2]{0,3,1,2:T(2,128)}), f32[9,1,128,2]{0,3,1,2:T(2,128)S(1)}, u32[]{:S(2)}, u32[]{:S(2)}) async-start(f32[9,1,128,2]{0,3,1,2:T(2,128)} %copy.182), calls=%async_computation.4 | async-start | bytes 262144 | tf_op jit(solution)/shard_map/all_to_all | solution.py:101
  170.0 69.0 %all-to-all-start.3 = ((f32[400,3,128,2]{0,3,1,2:T(2,128)}), f32[400,3,128,2]{0,3,1,2:T(2,128)}, u32[]{:S(2)}, u32[]{:S(2)}) async-start(f32[400,3,128,2]{0,3,1,2:T(2,128)} %copy.173), calls=%async_computation.3 | async-start | bytes 3145728 | tf_op jit(solution)/shard_map/all_to_all | solution.py:94
  177.6 47.3 %reduce-scatter.4.cloned.1.call-start = ((), (), s32[]{:S(2)}) async-start(), calls=%async_computation.6 | async-start | bytes 589824
  226.1 7.0 %collective-permute-start = (f32[3,128]{1,0:T(4,128)S(1)}, f32[3,128]{1,0:T(4,128)S(1)}, u32[]{:S(2)}, u32[]{:S(2)}) collective-permute-start(f32[3,128]{1,0:T(4,128)S(1)} %bitcast.129), channel_id=1, source_target_pairs={{0,8},{8,16},{16,24},{24,32},{32,40},{40,48},{48,56},{56,64},{64,7... | collective-permute-start | bytes 4616 | tf_op jit(solution)/shard_map/ppermute | solution.py:19
  230.8 7.6 %collective-permute-start.1 = (f32[3,128]{1,0:T(4,128)S(1)}, f32[3,128]{1,0:T(4,128)S(1)}, u32[]{:S(2)}, u32[]{:S(2)}) collective-permute-start(f32[3,128]{1,0:T(4,128)S(1)} %bitcast.130), channel_id=1, source_target_pairs={{8,0},{16,8},{24,16},{32,24},{40,32},{48,40},{56,48},{64,56},{72,6... | collective-permute-start | bytes 4616 | tf_op jit(solution)/shard_map/ppermute | solution.py:19
  (16 other events, 21.1 us)
Sparse Core Ops, SparseCore 0:
  192.4 32.4 reduce-scatter.3
where the time goes:
time: 252 us; the launch traced here: 251 us
  local copies, waits for them, and re-layouts  67 us (27%)
  waiting for transfers between devices  59.6 us (24%)
  matrix products  47.7 us (19%)
  starting transfers between devices  45.4 us (18%)
  other arithmetic  15.6 us (6%)
  between operations  14.5 us (6%)
    unnamed x2, waiting for transfers between devices  32.7 us
    dot_general x12, matrix products, sweep(): jnp.dot(stiff, current.reshape(grains, -1), precision=HIGHEST)  29.2 us
    while x60, local copies, waits for them, and re-layouts  17.7 us
    all_to_all x1, waiting for transfers between devices, per_device(): lax.all_to_all(send_disp, ('slab', 'helper'), split_axis=2, concat_axis=2...  15 us
    unnamed x31, local copies, waits for them, and re-layouts  12.4 us
    all_to_all x1, starting transfers between devices, per_device(): lax.all_to_all(send_counts, ('slab', 'helper'), split_axis=2, concat_axis...  10.5 us
    dot_general x1, matrix products, packing_stress(): jnp.einsum('gdp,gep->dep', internal, pos, precision=HIGHEST) / grains  10.4 us
    all_to_all x1, starting transfers between devices, per_device(): lax.all_to_all(send_disp, ('slab', 'helper'), split_axis=2, concat_axis=2...  10.2 us
  transfers between devices with their start and end apart: 8, of which 5 were waited for; matrix products, arithmetic and copies ran while one was open for 18% of the time, Pallas kernels for 0%

commit v1 on v0

v1 whole, which is shorter than its diff:
```python
import jax
import jax.numpy as jnp
from jax import lax
from jax.experimental import pallas as pl
from jax.experimental.pallas import tpu as pltpu
from jax.sharding import PartitionSpec as P

MESH = pl.DeviceIdType.MESH
GRAINS = 400
FLAT = 1200
POINTS = 128
SLOTS = 256
HELPERS = 8
SLABS = 16
DEVICES = 128
CHUNKS = 10
ROWS = 2 * CHUNKS
IT_HI = 12
F32 = jnp.float32
BF16 = jnp.bfloat16


def halves(x):
    hi = x.astype(BF16)
    lo = (x - hi.astype(F32)).astype(BF16)
    return hi, lo


def dot(a, b):
    return jnp.dot(a, b, preferred_element_type=F32)


def dot_nt(a, b):
    return lax.dot_general(a, b, (((1,), (1,)), ((), ())), preferred_element_type=F32)


def mixed(stiff, x):
    hi, lo = halves(x)
    return dot(stiff, hi) + dot(stiff, lo)


def at_device(index):
    return (index // HELPERS, lax.rem(index, HELPERS))


def kernel(
    cached_hbm, disp_hbm, mask_ref, strain_ref, counts_ref, assign_ref, node_ref, grads_ref,
    disp_out_hbm, stress_ref, grid_ref,
    cached, sent, got, part, sum_part, pos, stiff_ref, rate_ref, force,
    grid_out, own_got, low_got, high_got,
    load_sem, send_sem, recv_sem, own_sem, out_sem, grid_send, grid_recv,
):
    slab = lax.axis_index("slab")
    helper = lax.axis_index("helper")
    me = slab * HELPERS + helper

    load_cached = pltpu.make_async_copy(cached_hbm, cached, load_sem.at[0])
    load_cached.start()
    loads = []
    for d in range(3):
        copy = pltpu.make_async_copy(
            disp_hbm.at[pl.ds(d * GRAINS, GRAINS)],
            part.at[:, pl.ds(d * POINTS, POINTS)],
            load_sem.at[1 + d],
        )
        copy.start()
        loads.append(copy)

    barrier = pltpu.get_barrier_semaphore()

    def greet(step, carry):
        other = lax.rem(me + step, DEVICES)
        pl.semaphore_signal(barrier, inc=1, device_id=at_device(other), device_id_type=MESH)
        return carry

    lax.fori_loop(1, DEVICES, greet, 0)

    load_cached.wait()
    for k in range(CHUNKS):
        rows = min(128, FLAT - 128 * k)
        tile = cached[pl.ds(128 * k, rows), :]
        if rows < 128:
            tile = jnp.concatenate([tile, jnp.zeros((128 - rows, SLOTS), F32)], axis=0)
        sent[pl.ds(k, SLOTS, stride=CHUNKS), :] = tile.T

    pl.semaphore_wait(barrier, DEVICES - 1)

    def send(step, carry):
        other = lax.rem(me + step, DEVICES)
        pltpu.make_async_remote_copy(
            src_ref=sent.at[pl.ds(other * ROWS, ROWS)],
            dst_ref=got.at[pl.ds(me * ROWS, ROWS)],
            send_sem=send_sem,
            recv_sem=recv_sem,
            device_id=at_device(other),
            device_id_type=MESH,
        ).start()
        return carry

    lax.fori_loop(1, DEVICES, send, 0)
    own = pltpu.make_async_copy(
        sent.at[pl.ds(me * ROWS, ROWS)], got.at[pl.ds(me * ROWS, ROWS)], own_sem
    )
    own.start()

    stiff = mask_ref[...].astype(F32)
    scale = jnp.sum(stiff, axis=1, keepdims=True) + 1.0
    stiff_ref[...] = stiff.astype(BF16)
    rate_ref[...] = jnp.broadcast_to(0.8 / scale, (GRAINS, POINTS))
    counts = jnp.concatenate([counts_ref[...]] * 3, axis=1)

    def rate3():
        return jnp.concatenate([rate_ref[...]] * 3, axis=1)

    for copy in loads:
        copy.wait()

    def first(sweep, carry):
        u = part[...]
        new = 0.2 * u + rate3() * mixed(stiff_ref[...], u)
        part[...] = jnp.where(sweep < counts, new, u)
        return carry

    lax.fori_loop(0, IT_HI, first, 0)

    a_row = jnp.broadcast_to(assign_ref[...], (POINTS, POINTS))
    a_col = a_row.T
    p_at = lax.broadcasted_iota(jnp.int32, (POINTS, POINTS), 0)
    q_at = lax.broadcasted_iota(jnp.int32, (POINTS, POINTS), 1)
    rank = jnp.sum(
        jnp.where((a_row == a_col) & (q_at < p_at), 1.0, 0.0), axis=1, keepdims=True
    ).astype(jnp.int32)
    column = a_col * 2 + rank
    column = jnp.concatenate([column, column], axis=1)
    slot_at = lax.broadcasted_iota(jnp.int32, (POINTS, SLOTS), 1)
    pick = jnp.where(column == slot_at, 1.0, 0.0).astype(BF16)

    everything = sent.at[pl.ds(0, (DEVICES - 1) * ROWS)]
    own.wait()
    pltpu.make_async_copy(everything, everything, recv_sem).wait()

    for k in range(CHUNKS):
        hi, lo = halves(got[pl.ds(k, SLOTS, stride=CHUNKS), :])
        pos[pl.ds(128 * k, 128), :] = (dot(pick, hi) + dot(pick, lo)).T

    def position(e):
        return pos[pl.ds(e * GRAINS, GRAINS), :]

    for d in range(3):
        loading = sum(strain_ref[pl.ds(3 * d + e, 1), :] * position(e) for e in range(3))
        sum_part[:, pl.ds(d * POINTS, POINTS)] = rate_ref[...] * loading
    force[...] = sum_part[...]

    def second(sweep, carry):
        u = sum_part[...]
        new = 0.2 * u + rate3() * mixed(stiff_ref[...], u) + force[...]
        sum_part[...] = jnp.where(sweep < counts, new, u)
        return carry

    lax.fori_loop(1, IT_HI, second, 0)

    relaxed = part[...] + sum_part[...]
    part[...] = relaxed
    stores = []
    for d in range(3):
        copy = pltpu.make_async_copy(
            part.at[:, pl.ds(d * POINTS, POINTS)],
            disp_out_hbm.at[pl.ds(d * GRAINS, GRAINS)],
            out_sem.at[d],
        )
        copy.start()
        stores.append(copy)
    scale3 = 0.8 / rate3()
    internal = scale3 * relaxed - mixed(stiff_ref[...], relaxed)
    moments = [
        [
            jnp.sum(internal[:, d * POINTS : (d + 1) * POINTS] * position(e), axis=0, keepdims=True)
            / GRAINS
            for e in range(3)
        ]
        for d in range(3)
    ]
    stress = [[0.5 * (moments[d][e] + moments[e][d]) for e in range(3)] for d in range(3)]
    for d in range(3):
        for e in range(3):
            stress_ref[pl.ds(3 * d + e, 1), :] = stress[d][e]

    contrib = [-sum(stress[c][d] * grads_ref[d] for d in range(3)) for c in range(3)]
    row_at = lax.broadcasted_iota(jnp.int32, (128, POINTS), 0)
    total = jnp.zeros((128, 128), F32)
    for k in range(8):
        node = node_ref[pl.ds(k, 1), :]
        layer = node // 1024
        target = lax.rem(node, 1024) // 128
        low = lax.rem(node, 128)
        spread = jnp.where(row_at == low, 1.0, 0.0).astype(BF16)
        value = jnp.zeros((128, POINTS), F32)
        for c in range(3):
            value = jnp.where(row_at == target * 16 + layer * 4 + c, contrib[c][k : k + 1, :], value)
        hi, rest = halves(value)
        mid, low_part = halves(value - hi.astype(F32))
        total = total + dot_nt(hi, spread) + dot_nt(mid, spread) + dot_nt(low_part, spread)
    grid_out[...] = total
    below = lax.rem(slab + SLABS - 1, SLABS)
    above = lax.rem(slab + 1, SLABS)

    def grid_copy(first_row, count, kind, buffer, to_slab, to_helper):
        return pltpu.make_async_remote_copy(
            src_ref=grid_out.at[pl.ds(to_helper * 16 + first_row, count)],
            dst_ref=buffer.at[helper],
            send_sem=grid_send.at[kind],
            recv_sem=grid_recv.at[kind],
            device_id=(to_slab, to_helper),
            device_id_type=MESH,
        )

    def grid_sends(step, carry):
        to = lax.rem(helper + step, HELPERS)
        grid_copy(4, 8, 0, own_got, slab, to).start()
        return carry

    def grid_ghosts(step, carry):
        to = lax.rem(helper + step, HELPERS)
        grid_copy(0, 4, 1, high_got, below, to).start()
        grid_copy(12, 4, 2, low_got, above, to).start()
        return carry

    lax.fori_loop(0, HELPERS, grid_ghosts, 0)
    lax.fori_loop(1, HELPERS, grid_sends, 0)
    mine = pltpu.make_async_copy(
        grid_out.at[pl.ds(helper * 16 + 4, 8)], own_got.at[helper], own_sem
    )
    mine.start()
    mine.wait()
    pltpu.make_async_copy(high_got, high_got, grid_recv.at[1]).wait()
    pltpu.make_async_copy(low_got, low_got, grid_recv.at[2]).wait()
    seven = own_got.at[pl.ds(0, HELPERS - 1)]
    pltpu.make_async_copy(seven, seven, grid_recv.at[0]).wait()
    here = jnp.sum(own_got[...], axis=0)
    from_below = jnp.where(slab > 0, jnp.sum(low_got[...], axis=0), 0.0)
    from_above = jnp.where(slab < SLABS - 1, jnp.sum(high_got[...], axis=0), 0.0)
    grid_ref[...] = here + jnp.concatenate([from_below, from_above], axis=0)

    pltpu.make_async_copy(everything, everything, send_sem).wait()
    pltpu.make_async_copy(high_got, high_got, grid_send.at[1]).wait()
    pltpu.make_async_copy(low_got, low_got, grid_send.at[2]).wait()
    pltpu.make_async_copy(seven, seven, grid_send.at[0]).wait()
    for copy in stores:
        copy.wait()


def per_device(disp, strain, counts, assign, cached_pos, contact_mask, node_index, node_grads):
    vmem = pl.BlockSpec(memory_space=pltpu.VMEM)
    hbm = pl.BlockSpec(memory_space=pl.ANY)
    disp_out, stress, grid = pl.pallas_call(
        kernel,
        out_shape=(
            jax.ShapeDtypeStruct((FLAT, POINTS), F32),
            jax.ShapeDtypeStruct((9, POINTS), F32),
            jax.ShapeDtypeStruct((8, 128), F32),
        ),
        in_specs=[hbm, hbm, vmem, vmem, vmem, vmem, vmem, vmem],
        out_specs=(hbm, vmem, vmem),
        scratch_shapes=[
            pltpu.VMEM((FLAT, SLOTS), F32),
            pltpu.VMEM((DEVICES * ROWS, 128), F32),
            pltpu.VMEM((DEVICES * ROWS, 128), F32),
            pltpu.VMEM((GRAINS, 3 * POINTS), F32),
            pltpu.VMEM((GRAINS, 3 * POINTS), F32),
            pltpu.VMEM((128 * CHUNKS, POINTS), F32),
            pltpu.VMEM((GRAINS, GRAINS), BF16),
            pltpu.VMEM((GRAINS, POINTS), F32),
            pltpu.VMEM((GRAINS, 3 * POINTS), F32),
            pltpu.VMEM((128, 128), F32),
            pltpu.VMEM((HELPERS, 8, 128), F32),
            pltpu.VMEM((HELPERS, 4, 128), F32),
            pltpu.VMEM((HELPERS, 4, 128), F32),
            pltpu.SemaphoreType.DMA((4,)),
            pltpu.SemaphoreType.DMA,
            pltpu.SemaphoreType.DMA,
            pltpu.SemaphoreType.DMA,
            pltpu.SemaphoreType.DMA((3,)),
            pltpu.SemaphoreType.DMA((3,)),
            pltpu.SemaphoreType.DMA((3,)),
        ],
        compiler_params=pltpu.CompilerParams(
            collective_id=0, has_side_effects=True, vmem_limit_bytes=48 << 20
        ),
    )(
        cached_pos.transpose(1, 0, 2).reshape(FLAT, SLOTS),
        disp.transpose(1, 0, 2).reshape(FLAT, POINTS),
        contact_mask,
        strain,
        counts.reshape(1, POINTS),
        assign.reshape(1, POINTS),
        node_index,
        node_grads,
    )
    return (
        disp_out.reshape(3, GRAINS, POINTS).transpose(1, 0, 2),
        stress,
        grid.reshape(2, 4, 128)[:, :3].transpose(1, 0, 2),
    )


def solution(mesh):
    both = ("slab", "helper")
    return jax.shard_map(
        per_device,
        mesh=mesh,
        in_specs=(
            P(None, None, both),
            P(None, both),
            P(both),
            P(both, None),
            P(None, None, both),
            P(),
            P(None, both),
            P(None, None, both),
        ),
        out_specs=(P(None, None, both), P(None, both), P(None, "slab", "helper")),
        check_vma=False,
    )
```

time: 252 us -> 58.7 us (0.23)
  the two profiles are of different devices: /device:TPU:6 before, /device:TPU:1 now
where the time goes in v1:
time: 58.7 us; the launch traced here: 58.4 us
  Pallas kernels  48.8 us (83%)
  local copies, waits for them, and re-layouts  8.9 us (15%)
  between operations  0.66 us (1%)
    pallas_call x1, Pallas kernels, per_device(): pl.pallas_call(kernel, out_shape=(jax.ShapeDtypeStruct((FLAT, POINTS), F3...  48.8 us
    unnamed x19, local copies, waits for them, and re-layouts  8.9 us

profile of v1, /device:TPU:1, one launch (start us, length us, event | category | flops | bytes accessed | tf_op | source)
XLA Modules:
  0.0 58.4 jit_solution(16841937006825047587)
XLA Ops:
  0.6 0.0 copy-start
  0.6 1.3 %copy-done = f32[400,3,256]{2,0,1:T(8,128)S(1)} copy-done((f32[400,3,256]{2,0,1:T(8,128)S(1)}, f32[400,3,256]{2,0,1:T(8,128)}, u32[]{:S(2)}) %copy-start) | copy-done | bytes 1228824
  1.9 0.0 copy-start.1
  1.9 1.1 %copy-done.1 = s32[400,400]{1,0:T(8,128)S(1)} copy-done((s32[400,400]{1,0:T(8,128)S(1)}, s32[400,400]{1,0:T(8,128)}, u32[]{:S(2)}) %copy-start.1) | copy-done | bytes 640024
  3.1 0.0 copy-start.2
  3.1 1.1 %copy-done.2 = f32[400,3,128]{2,0,1:T(8,128)S(1)} copy-done((f32[400,3,128]{2,0,1:T(8,128)S(1)}, f32[400,3,128]{2,0,1:T(8,128)}, u32[]{:S(2)}) %copy-start.2) | copy-done | bytes 614424
  4.1 0.0 copy-start.3
  4.1 0.7 %copy-done.3 = f32[3,8,128]{2,1,0:T(8,128)S(1)} copy-done((f32[3,8,128]{2,1,0:T(8,128)S(1)}, f32[3,8,128]{2,1,0:T(8,128)}, u32[]{:S(2)}) %copy-start.3) | copy-done | bytes 12312
  4.8 0.0 copy-start.4
  4.8 0.7 %copy-done.4 = f32[9,128]{1,0:T(8,128)S(1)} copy-done((f32[9,128]{1,0:T(8,128)S(1)}, f32[9,128]{1,0:T(8,128)}, u32[]{:S(2)}) %copy-start.4) | copy-done | bytes 4632
  5.5 0.0 copy-start.5
  5.5 0.7 %copy-done.5 = s32[8,128]{1,0:T(8,128)S(1)} copy-done((s32[8,128]{1,0:T(8,128)S(1)}, s32[8,128]{1,0:T(8,128)}, u32[]{:S(2)}) %copy-start.5) | copy-done | bytes 4120
  6.2 0.0 copy-start.6
  6.2 0.7 %copy-done.6 = s32[128]{0:T(128)S(1)} copy-done((s32[128]{0:T(128)S(1)}, s32[128]{0:T(128)}, u32[]{:S(2)}) %copy-start.6) | copy-done | bytes 536
  6.9 0.0 copy-start.7
  6.9 0.7 %copy-done.7 = s32[128,1]{0,1:T(1,128)S(1)} copy-done((s32[128,1]{0,1:T(1,128)S(1)}, s32[128,1]{0,1:T(1,128)}, u32[]{:S(2)}) %copy-start.7) | copy-done | bytes 536
  7.5 48.8 %shard_map.103 = (f32[1200,128]{1,0:T(8,128)S(1)}, f32[9,128]{1,0:T(8,128)S(1)}, f32[8,128]{1,0:T(8,128)S(1)}) custom-call(f32[1200,256]{1,0:T(8,128)S(1)} %bitcast.16, f32[1200,128]{1,0:T(8,128)S(1)} %bitcast.17, s32[400,400]{1,0:T(8,128)S(1)} %copy-done.1, f32[9,128]{1,0:T(8,128)S(1)} %copy-done.4, s32[1,128]{1,0:T(1,128)S(1)} %bitcast.20, ...), custom_call_target="tpu_custom_call" | custom-call | tf_op jit(solution)/shard_map/pallas_call | solution.py:255
  56.4 0.6 copy.14
  56.9 0.8 %copy.17 = f32[400,3,128]{2,0,1:T(8,128)} copy(f32[400,3,128]{2,0,1:T(8,128)S(1)} %bitcast.18) | data formatting | bytes 1228800
  57.8 0.6 %copy.18 = f32[9,128]{1,0:T(8,128)} copy(f32[9,128]{1,0:T(8,128)S(1)} %get-tuple-element.13) | data formatting | bytes 9216
Async XLA Ops:
  0.6 1.3 %copy-start = (f32[400,3,256]{2,0,1:T(8,128)S(1)}, f32[400,3,256]{2,0,1:T(8,128)}, u32[]{:S(2)}) copy-start(f32[400,3,256]{2,0,1:T(8,128)} %param.12) | copy-start | bytes 3686404
  1.9 1.1 %copy-start.1 = (s32[400,400]{1,0:T(8,128)S(1)}, s32[400,400]{1,0:T(8,128)}, u32[]{:S(2)}) copy-start(s32[400,400]{1,0:T(8,128)} %mask_ref.1) | copy-start | bytes 1920004
  3.1 1.1 %copy-start.2 = (f32[400,3,128]{2,0,1:T(8,128)S(1)}, f32[400,3,128]{2,0,1:T(8,128)}, u32[]{:S(2)}) copy-start(f32[400,3,128]{2,0,1:T(8,128)} %param.8) | copy-start | bytes 1843204
  4.1 0.7 %copy-start.3 = (f32[3,8,128]{2,1,0:T(8,128)S(1)}, f32[3,8,128]{2,1,0:T(8,128)}, u32[]{:S(2)}) copy-start(f32[3,8,128]{2,1,0:T(8,128)} %grads_ref.1) | copy-start | bytes 36868
  4.8 0.7 %copy-start.4 = (f32[9,128]{1,0:T(8,128)S(1)}, f32[9,128]{1,0:T(8,128)}, u32[]{:S(2)}) copy-start(f32[9,128]{1,0:T(8,128)} %strain_ref.1) | copy-start | bytes 13828
  5.5 0.7 %copy-start.5 = (s32[8,128]{1,0:T(8,128)S(1)}, s32[8,128]{1,0:T(8,128)}, u32[]{:S(2)}) copy-start(s32[8,128]{1,0:T(8,128)} %node_ref.1) | copy-start | bytes 12292
  6.2 0.7 %copy-start.6 = (s32[128]{0:T(128)S(1)}, s32[128]{0:T(128)}, u32[]{:S(2)}) copy-start(s32[128]{0:T(128)} %param.10) | copy-start | bytes 1540
  6.9 0.7 %copy-start.7 = (s32[128,1]{0,1:T(1,128)S(1)}, s32[128,1]{0,1:T(1,128)}, u32[]{:S(2)}) copy-start(s32[128,1]{0,1:T(1,128)} %param.11) | copy-start | bytes 1540

commit v2 on v1

v2 whole, which is shorter than its diff:
```python
import itertools

import jax
import jax.numpy as jnp
from jax import lax
from jax.experimental import pallas as pl
from jax.experimental.pallas import tpu as pltpu
from jax.sharding import PartitionSpec as P

MESH = pl.DeviceIdType.MESH
GRAINS = 400
FLAT = 1200
POINTS = 128
WIDE = 3 * POINTS
SLOTS = 256
HELPERS = 8
SLABS = 16
DEVICES = 128
CHUNKS = 10
ROWS = 2 * CHUNKS
CORNERS = 8
BABY = 4
GIANT = 3
F32 = jnp.float32
BF16 = jnp.bfloat16


def halves(x):
    hi = x.astype(BF16)
    lo = (x - hi.astype(F32)).astype(BF16)
    return hi, lo


def dot(a, b):
    return jnp.dot(a, b, preferred_element_type=F32)


def dot3(a, b):
    return dot(a[0], b[0]) + dot(a[0], b[1]) + dot(a[1], b[0])


def dot_nt(a, b):
    return lax.dot_general(a, b, (((1,), (1,)), ((), ())), preferred_element_type=F32)


def ring(a):
    return min(a, 4 - a)


OFFSETS = sorted(
    (
        offset
        for offset in itertools.product(range(4), range(4), range(4), range(2))
        if any(offset)
    ),
    key=lambda o: (-ring(o[0]) - ring(o[1]) - ring(o[2]), (o[0] * 5 + o[1] * 11 + o[2] * 3 + o[3] * 7) % 13),
)


def kernel(
    cached_hbm, disp_hbm, mask_hbm, strain_hbm, counts_hbm, assign_hbm, node_hbm, grads_hbm,
    disp_out, stress_ref, grid_ref,
    cached, disp, mask, strain, counts_ref, assign, node, grads,
    sent, got, part, pos, steps_hi, steps_lo, giant_hi, giant_lo, hit, spread,
    grid_out, own_got, low_got, high_got,
    load_sem, send_sem, recv_sem, own_sem, grid_send, grid_recv,
):
    slab = lax.axis_index("slab")
    helper = lax.axis_index("helper")
    me = slab * HELPERS + helper

    moves = [(cached_hbm, cached)]
    for d in range(3):
        moves.append(
            (disp_hbm.at[pl.ds(d * GRAINS, GRAINS)], disp.at[:, pl.ds(d * POINTS, POINTS)])
        )
    moves += [
        (mask_hbm, mask), (strain_hbm, strain), (counts_hbm, counts_ref),
        (assign_hbm, assign), (node_hbm, node), (grads_hbm, grads),
    ]
    loads = [
        pltpu.make_async_copy(source, target, load_sem.at[i])
        for i, (source, target) in enumerate(moves)
    ]
    for copy in loads:
        copy.start()

    z, x, y, core = slab // 4, lax.rem(slab, 4), helper // 2, lax.rem(helper, 2)
    slab_at = {
        (a, b): lax.rem(z + a, 4) * 4 + lax.rem(x + b, 4) for a in range(4) for b in range(4)
    }
    helper_at = {
        (a, b): lax.rem(y + a, 4) * 2 + lax.rem(core + b, 2) for a in range(4) for b in range(2)
    }
    others = [(slab_at[o[:2]], helper_at[o[2:]]) for o in OFFSETS]

    barrier = pltpu.get_barrier_semaphore()
    for other in others:
        pl.semaphore_signal(barrier, inc=1, device_id=other, device_id_type=MESH)

    loads[0].wait()
    for k in range(CHUNKS):
        rows = min(128, FLAT - 128 * k)
        tile = cached[pl.ds(128 * k, rows), :]
        if rows < 128:
            tile = jnp.concatenate([tile, jnp.zeros((128 - rows, SLOTS), F32)], axis=0)
        sent[pl.ds(k, SLOTS, stride=CHUNKS), :] = tile.T

    pl.semaphore_wait(barrier, DEVICES - 1)

    for to_slab, to_helper in others:
        pltpu.make_async_remote_copy(
            src_ref=sent.at[pl.ds((to_slab * HELPERS + to_helper) * ROWS, ROWS)],
            dst_ref=got.at[pl.ds(me * ROWS, ROWS)],
            send_sem=send_sem,
            recv_sem=recv_sem,
            device_id=(to_slab, to_helper),
            device_id_type=MESH,
        ).start()
    own = pltpu.make_async_copy(
        sent.at[pl.ds(me * ROWS, ROWS)], got.at[pl.ds(me * ROWS, ROWS)], own_sem
    )
    own.start()

    for copy in loads[1:]:
        copy.wait()

    stiff = mask[...].astype(F32)
    scale = jnp.sum(stiff, axis=1, keepdims=True) + 1.0
    rate = 0.8 / scale
    rate_row = 0.8 / (jnp.sum(stiff, axis=0, keepdims=True) + 1.0)
    g_at = lax.broadcasted_iota(jnp.int32, (GRAINS, GRAINS), 0)
    h_at = lax.broadcasted_iota(jnp.int32, (GRAINS, GRAINS), 1)
    once = jnp.where(g_at == h_at, 0.2, 0.0) + rate * stiff
    once_h = halves(once)
    twice = dot3(once_h, once_h)
    twice_h = halves(twice)
    thrice = dot3(twice_h, once_h)
    hi, lo = halves(dot3(twice_h, twice_h))
    giant_hi[...] = hi
    giant_lo[...] = lo
    for i, power in enumerate((once, twice, thrice)):
        hi, lo = halves(power * rate_row)
        steps_hi[pl.ds(i * GRAINS, GRAINS), :] = hi
        steps_lo[pl.ds(i * GRAINS, GRAINS), :] = lo
    steps_hi[pl.ds(3 * GRAINS, GRAINS), :] = stiff.astype(BF16)

    def stepped(x_h, i):
        rows = pl.ds(i * GRAINS, GRAINS)
        return dot3((steps_hi[rows, :], steps_lo[rows, :]), x_h)

    def leap(x):
        return dot3((giant_hi[...], giant_lo[...]), halves(x))

    counts = jnp.concatenate([counts_ref[...]] * 3, axis=1)
    start = disp[...]
    start_h = halves(start * (1.25 * scale))
    powers = [start] + [stepped(start_h, i) for i in range(BABY - 1)]
    total = jnp.where(counts == BABY * GIANT, start, 0.0)
    for j in reversed(range(GIANT)):
        term = jnp.zeros((GRAINS, WIDE), F32)
        for i in range(BABY):
            term = jnp.where(counts == BABY * j + i, powers[i], term)
        total = term + leap(total)
    part[...] = total

    a_row = jnp.broadcast_to(assign[...], (POINTS, POINTS))
    a_col = a_row.T
    p_at = lax.broadcasted_iota(jnp.int32, (POINTS, POINTS), 0)
    q_at = lax.broadcasted_iota(jnp.int32, (POINTS, POINTS), 1)
    rank = jnp.sum(
        jnp.where((a_row == a_col) & (q_at < p_at), 1.0, 0.0), axis=1, keepdims=True
    ).astype(jnp.int32)
    column = a_col * 2 + rank
    column = jnp.concatenate([column, column], axis=1)
    slot_at = lax.broadcasted_iota(jnp.int32, (POINTS, SLOTS), 1)
    pick = jnp.where(column == slot_at, 1.0, 0.0).astype(BF16)

    for k in range(CORNERS):
        at = node[pl.ds(k, 1), :]
        layer = at // 1024
        target = lax.rem(at, 1024) // 128
        low = lax.rem(at, 128)
        lanes = pl.ds(k * POINTS, POINTS)
        spread[:, lanes] = jnp.where(p_at == low, 1.0, 0.0).astype(BF16)
        hit[:, lanes] = jnp.where(p_at // 4 == target * 4 + layer, 1.0, 0.0)

    everything = sent.at[pl.ds(0, (DEVICES - 1) * ROWS)]
    own.wait()
    pltpu.make_async_copy(everything, everything, recv_sem).wait()

    for k in range(CHUNKS):
        hi, lo = halves(got[pl.ds(k, SLOTS, stride=CHUNKS), :])
        tile = (dot(pick, hi) + dot(pick, lo)).T
        first = 128 * k
        while first < min(128 * k + 128, FLAT):
            e = first // GRAINS
            last = min(128 * k + 128, (e + 1) * GRAINS)
            pos[pl.ds(first - e * GRAINS, last - first), pl.ds(e * POINTS, POINTS)] = tile[
                first - 128 * k : last - 128 * k
            ]
            first = last

    place = pos[...]
    place_h = halves(place)
    powers = [rate * place] + [stepped(place_h, i) for i in range(BABY - 1)]
    contact = steps_hi[pl.ds(3 * GRAINS, GRAINS), :]
    pull = scale * place - (dot(contact, place_h[0]) + dot(contact, place_h[1]))
    total = None
    for j in reversed(range(GIANT)):
        term = jnp.zeros((GRAINS, WIDE), F32)
        for i in range(BABY):
            term = term + jnp.where(BABY * j + i < counts, powers[i], 0.0)
        total = term if total is None else term + leap(total)

    def across(x, e):
        return x[:, e * POINTS : (e + 1) * POINTS]

    relaxed = [
        part[:, pl.ds(d * POINTS, POINTS)]
        + sum(strain[pl.ds(3 * d + e, 1), :] * across(total, e) for e in range(3))
        for d in range(3)
    ]
    for d in range(3):
        disp_out[pl.ds(d * GRAINS, GRAINS), :] = relaxed[d]
    moments = [
        [jnp.sum(relaxed[d] * across(pull, e), axis=0, keepdims=True) / GRAINS for e in range(3)]
        for d in range(3)
    ]
    stress = [[0.5 * (moments[d][e] + moments[e][d]) for e in range(3)] for d in range(3)]
    for d in range(3):
        for e in range(3):
            stress_ref[pl.ds(3 * d + e, 1), :] = stress[d][e]

    nothing = jnp.zeros((1, POINTS), F32)
    rows = [
        jnp.concatenate([stress[0][d], stress[1][d], stress[2][d], nothing] * 2, axis=0)
        for d in range(3)
    ]
    contrib = jnp.concatenate(
        [-sum(rows[d] * grads[d, pl.ds(k, 1), :] for d in range(3)) for k in range(CORNERS)], axis=1
    )
    hi, lo = halves(jnp.concatenate([contrib] * 16, axis=0) * hit[...])
    grid_out[...] = dot_nt(hi, spread[...]) + dot_nt(lo, spread[...])
    below = lax.rem(slab + SLABS - 1, SLABS)
    above = lax.rem(slab + 1, SLABS)

    def grid_copy(first_row, count, kind, buffer, to_slab, to_helper):
        return pltpu.make_async_remote_copy(
            src_ref=grid_out.at[pl.ds(to_helper * 16 + first_row, count)],
            dst_ref=buffer.at[helper],
            send_sem=grid_send.at[kind],
            recv_sem=grid_recv.at[kind],
            device_id=(to_slab, to_helper),
            device_id_type=MESH,
        )

    for step in range(HELPERS):
        to = lax.rem(helper + step, HELPERS)
        grid_copy(0, 4, 1, high_got, below, to).start()
        grid_copy(12, 4, 2, low_got, above, to).start()
        if step:
            grid_copy(4, 8, 0, own_got, slab, to).start()
    mine = pltpu.make_async_copy(
        grid_out.at[pl.ds(helper * 16 + 4, 8)], own_got.at[helper], own_sem
    )
    mine.start()
    mine.wait()
    pltpu.make_async_copy(high_got, high_got, grid_recv.at[1]).wait()
    pltpu.make_async_copy(low_got, low_got, grid_recv.at[2]).wait()
    seven = own_got.at[pl.ds(0, HELPERS - 1)]
    pltpu.make_async_copy(seven, seven, grid_recv.at[0]).wait()
    here = jnp.sum(own_got[...], axis=0)
    from_below = jnp.where(slab > 0, jnp.sum(low_got[...], axis=0), 0.0)
    from_above = jnp.where(slab < SLABS - 1, jnp.sum(high_got[...], axis=0), 0.0)
    here = here + jnp.concatenate([from_below, from_above], axis=0)
    for c in range(3):
        for layer in range(2):
            grid_ref[c, pl.ds(layer, 1), :] = here[4 * layer + c : 4 * layer + c + 1]

    pltpu.make_async_copy(everything, everything, send_sem).wait()
    pltpu.make_async_copy(high_got, high_got, grid_send.at[1]).wait()
    pltpu.make_async_copy(low_got, low_got, grid_send.at[2]).wait()
    pltpu.make_async_copy(seven, seven, grid_send.at[0]).wait()


PIECES = 6


def hand_over(disp_in, stress_in, grid_in, disp_out, stress_out, grid_out, sems):
    rows = FLAT // PIECES
    copies = [
        pltpu.make_async_copy(
            disp_in.at[pl.ds(i * rows, rows)], disp_out.at[pl.ds(i * rows, rows)], sems.at[i]
        )
        for i in range(PIECES)
    ]
    copies.append(pltpu.make_async_copy(stress_in, stress_out, sems.at[PIECES]))
    copies.append(pltpu.make_async_copy(grid_in, grid_out, sems.at[PIECES + 1]))
    for copy in copies:
        copy.start()
    for copy in copies:
        copy.wait()


def per_device(disp, strain, counts, assign, cached_pos, contact_mask, node_index, node_grads):
    vmem = pl.BlockSpec(memory_space=pltpu.VMEM)
    hbm = pl.BlockSpec(memory_space=pltpu.MemorySpace.HBM)
    shapes = ((FLAT, POINTS), (9, POINTS), (3, 2, 128))

    def keep(x):
        return pltpu.with_memory_space_constraint(x, pltpu.MemorySpace.HBM)

    outs = pl.pallas_call(
        kernel,
        out_shape=tuple(pltpu.VMEM(shape, F32) for shape in shapes),
        in_specs=[hbm] * 8,
        out_specs=(vmem,) * 3,
        scratch_shapes=[
            pltpu.VMEM((FLAT, SLOTS), F32),
            pltpu.VMEM((GRAINS, WIDE), F32),
            pltpu.VMEM((GRAINS, GRAINS), jnp.int32),
            pltpu.VMEM((9, POINTS), F32),
            pltpu.VMEM((1, POINTS), jnp.int32),
            pltpu.VMEM((1, POINTS), jnp.int32),
            pltpu.VMEM((CORNERS, POINTS), jnp.int32),
            pltpu.VMEM((3, CORNERS, POINTS), F32),
            pltpu.VMEM((DEVICES * ROWS, 128), F32),
            pltpu.VMEM((DEVICES * ROWS, 128), F32),
            pltpu.VMEM((GRAINS, WIDE), F32),
            pltpu.VMEM((GRAINS, WIDE), F32),
            pltpu.VMEM((4 * GRAINS, GRAINS), BF16),
            pltpu.VMEM((3 * GRAINS, GRAINS), BF16),
            pltpu.VMEM((GRAINS, GRAINS), BF16),
            pltpu.VMEM((GRAINS, GRAINS), BF16),
            pltpu.VMEM((128, CORNERS * POINTS), F32),
            pltpu.VMEM((128, CORNERS * POINTS), BF16),
            pltpu.VMEM((128, 128), F32),
            pltpu.VMEM((HELPERS, 8, 128), F32),
            pltpu.VMEM((HELPERS, 4, 128), F32),
            pltpu.VMEM((HELPERS, 4, 128), F32),
            pltpu.SemaphoreType.DMA((10,)),
            pltpu.SemaphoreType.DMA,
            pltpu.SemaphoreType.DMA,
            pltpu.SemaphoreType.DMA,
            pltpu.SemaphoreType.DMA((3,)),
            pltpu.SemaphoreType.DMA((3,)),
        ],
        compiler_params=pltpu.CompilerParams(
            collective_id=0, has_side_effects=True, vmem_limit_bytes=56 << 20
        ),
    )(
        keep(cached_pos.transpose(1, 0, 2).reshape(FLAT, SLOTS)),
        keep(disp.transpose(1, 0, 2).reshape(FLAT, POINTS)),
        keep(contact_mask),
        keep(strain),
        keep(counts.reshape(1, POINTS)),
        keep(assign.reshape(1, POINTS)),
        keep(node_index),
        keep(node_grads),
    )
    disp_out, stress, grid = pl.pallas_call(
        hand_over,
        out_shape=tuple(jax.ShapeDtypeStruct(shape, F32) for shape in shapes),
        in_specs=[vmem] * 3,
        out_specs=(hbm,) * 3,
        scratch_shapes=[pltpu.SemaphoreType.DMA((PIECES + 2,))],
    )(*outs)
    return disp_out.reshape(3, GRAINS, POINTS).transpose(1, 0, 2), stress, grid


def solution(mesh):
    both = ("slab", "helper")
    return jax.shard_map(
        per_device,
        mesh=mesh,
        in_specs=(
            P(None, None, both),
            P(None, both),
            P(both),
            P(both, None),
            P(None, None, both),
            P(),
            P(None, both),
            P(None, None, both),
        ),
        out_specs=(P(None, None, both), P(None, both), P(None, "slab", "helper")),
        check_vma=False,
    )
```

time: 58.7 us -> 42.7 us (0.73)
  Pallas kernels: 48.8 us -> 39.9 us
  local copies, waits for them, and re-layouts: 8.9 us -> 2.02 us
    pallas_call x1 -> x2, Pallas kernels: 48.8 us -> 39.9 us  [the longest x1 38 us: per_device(): pl.pallas_call(kernel, out_shape=tuple((pltpu.VMEM(shape, F32) for shape...]
    unnamed x19 -> x6, local copies, waits for them, and re-layouts: 8.9 us -> 2.02 us
where the time goes in v2:
time: 42.7 us; the launch traced here: 42.6 us
  Pallas kernels  39.9 us (93%)
  local copies, waits for them, and re-layouts  2.02 us (5%)
  between operations  0.65 us (2%)
    pallas_call x1, Pallas kernels, per_device(): pl.pallas_call(kernel, out_shape=tuple((pltpu.VMEM(shape, F32) for shape...  38 us
    unnamed x6, local copies, waits for them, and re-layouts  2.02 us
    pallas_call x1, Pallas kernels, per_device(): pl.pallas_call(hand_over, out_shape=tuple((jax.ShapeDtypeStruct(shape, F3...  1.97 us

profile of v2, /device:TPU:1, one launch (start us, length us, event | category | flops | bytes accessed | tf_op | source)
XLA Modules:
  0.0 42.6 jit_solution(3095039259982808834)
XLA Ops:
  0.6 38.0 %shard_map.103 = (f32[1200,128]{1,0:T(8,128)S(1)}, f32[9,128]{1,0:T(8,128)S(1)}, f32[3,2,128]{2,1,0:T(2,128)S(1)}) custom-call(f32[1200,256]{1,0:T(8,128)} %bitcast.11, f32[1200,128]{1,0:T(8,128)} %bitcast.12, s32[400,400]{1,0:T(8,128)} %mask_hbm.1, f32[9,128]{1,0:T(8,128)} %strain_hbm.1, s32[1,128]{1,0:T(1,128)} %bitcast.13, s32[1,128]{1,0:T(1,128)} %bitcast.14, ...), custom_call_target="tpu_custom_call" | custom-call | tf_op jit(solution)/shard_map/pallas_call | solution.py:314
  38.6 0.0 copy-start
  38.6 0.8 %copy-done = f32[1200,128]{1,0:T(8,128)} copy-done((f32[1200,128]{1,0:T(8,128)}, f32[1200,128]{1,0:T(8,128)S(1)}, u32[]{:S(2)}) %copy-start) | copy-done | bytes 614424
  39.4 0.0 copy-start.1
  39.4 0.6 %copy-done.1 = f32[9,128]{1,0:T(8,128)} copy-done((f32[9,128]{1,0:T(8,128)}, f32[9,128]{1,0:T(8,128)S(1)}, u32[]{:S(2)}) %copy-start.1) | copy-done | bytes 4632
  40.0 0.0 copy-start.2
  40.0 0.6 %copy-done.2 = f32[3,2,128]{2,1,0:T(2,128)} copy-done((f32[3,2,128]{2,1,0:T(2,128)}, f32[3,2,128]{2,1,0:T(2,128)S(1)}, u32[]{:S(2)}) %copy-start.2) | copy-done | bytes 3096
  40.6 2.0 %shard_map.104 = (f32[1200,128]{1,0:T(8,128)}, f32[9,128]{1,0:T(8,128)}, f32[3,2,128]{2,1,0:T(2,128)}) custom-call(f32[1200,128]{1,0:T(8,128)} %copy-done, f32[9,128]{1,0:T(8,128)} %copy-done.1, f32[3,2,128]{2,1,0:T(2,128)} %copy-done.2), custom_call_target="tpu_custom_call" | custom-call | tf_op jit(solution)/shard_map/pallas_call | solution.py:362
Async XLA Ops:
  38.6 0.8 %copy-start = (f32[1200,128]{1,0:T(8,128)}, f32[1200,128]{1,0:T(8,128)S(1)}, u32[]{:S(2)}) copy-start(f32[1200,128]{1,0:T(8,128)S(1)} %get-tuple-element.9.disp_in) | copy-start | bytes 1843204
  39.4 0.6 %copy-start.1 = (f32[9,128]{1,0:T(8,128)}, f32[9,128]{1,0:T(8,128)S(1)}, u32[]{:S(2)}) copy-start(f32[9,128]{1,0:T(8,128)S(1)} %get-tuple-element.10.stress_in) | copy-start | bytes 13828
  40.0 0.6 %copy-start.2 = (f32[3,2,128]{2,1,0:T(2,128)}, f32[3,2,128]{2,1,0:T(2,128)S(1)}, u32[]{:S(2)}) copy-start(f32[3,2,128]{2,1,0:T(2,128)S(1)} %get-tuple-element.11.grid_in) | copy-start | bytes 9220

commit v3 on v2

--- a/solution.py
+++ b/solution.py
@@ -16,8 +16,9 @@
 HELPERS = 8
 SLABS = 16
 DEVICES = 128
-CHUNKS = 10
-ROWS = 2 * CHUNKS
+FULL = FLAT // 128
+TAIL = FLAT - 128 * FULL
+ROWS = 2 * FULL + 1
 CORNERS = 8
 BABY = 4
 GIANT = 3
@@ -35,8 +36,14 @@
     return jnp.dot(a, b, preferred_element_type=F32)
 
 
+def dot2(a, b):
+    width = b[0].shape[1]
+    both = dot(a, jnp.concatenate(b, axis=1))
+    return both[:, :width] + both[:, width:]
+
+
 def dot3(a, b):
-    return dot(a[0], b[0]) + dot(a[0], b[1]) + dot(a[1], b[0])
+    return dot2(a[0], b) + dot(a[1], b[0])
 
 
 def dot_nt(a, b):
@@ -61,7 +68,7 @@
     cached_hbm, disp_hbm, mask_hbm, strain_hbm, counts_hbm, assign_hbm, node_hbm, grads_hbm,
     disp_out, stress_ref, grid_ref,
     cached, disp, mask, strain, counts_ref, assign, node, grads,
-    sent, got, part, pos, steps_hi, steps_lo, giant_hi, giant_lo, hit, spread,
+    turned, sent, got, part, pos, steps_hi, steps_lo, giant_hi, giant_lo, hit, spread,
     grid_out, own_got, low_got, high_got,
     load_sem, send_sem, recv_sem, own_sem, grid_send, grid_recv,
 ):
@@ -99,12 +106,19 @@
         pl.semaphore_signal(barrier, inc=1, device_id=other, device_id_type=MESH)
 
     loads[0].wait()
-    for k in range(CHUNKS):
-        rows = min(128, FLAT - 128 * k)
-        tile = cached[pl.ds(128 * k, rows), :]
-        if rows < 128:
-            tile = jnp.concatenate([tile, jnp.zeros((128 - rows, SLOTS), F32)], axis=0)
-        sent[pl.ds(k, SLOTS, stride=CHUNKS), :] = tile.T
+    for k in range(FULL):
+        turned[k] = cached[pl.ds(128 * k, 128), :].T
+    for k in range(FULL):
+        for c in range(2):
+            sent[pl.ds(FULL * c + k, DEVICES, stride=ROWS), :] = turned[
+                k, pl.ds(c, DEVICES, stride=2), :
+            ]
+    tail = cached[pl.ds(128 * FULL, TAIL), :]
+    turned[0] = jnp.concatenate([tail, tail, jnp.zeros((128 - 2 * TAIL, SLOTS), F32)], axis=0).T
+    lane = lax.broadcasted_iota(jnp.int32, (DEVICES, 128), 1)
+    sent[pl.ds(2 * FULL, DEVICES, stride=ROWS), :] = jnp.where(
+        lane < TAIL, turned[0, pl.ds(0, DEVICES, stride=2), :], turned[0, pl.ds(1, DEVICES, stride=2), :]
+    )
 
     pl.semaphore_wait(barrier, DEVICES - 1)
 
@@ -136,9 +150,10 @@
     twice = dot3(once_h, once_h)
     twice_h = halves(twice)
     thrice = dot3(twice_h, once_h)
-    hi, lo = halves(dot3(twice_h, twice_h))
-    giant_hi[...] = hi
-    giant_lo[...] = lo
+    leap_h = halves(dot3(twice_h, twice_h))
+    for i, power in enumerate((leap_h, halves(dot3(leap_h, leap_h)))):
+        giant_hi[i] = power[0]
+        giant_lo[i] = power[1]
     for i, power in enumerate((once, twice, thrice)):
         hi, lo = halves(power * rate_row)
         steps_hi[pl.ds(i * GRAINS, GRAINS), :] = hi
@@ -149,20 +164,21 @@
         rows = pl.ds(i * GRAINS, GRAINS)
         return dot3((steps_hi[rows, :], steps_lo[rows, :]), x_h)
 
-    def leap(x):
-        return dot3((giant_hi[...], giant_lo[...]), halves(x))
+    def leap(i, x):
+        return dot3((giant_hi[i], giant_lo[i]), halves(x))
 
     counts = jnp.concatenate([counts_ref[...]] * 3, axis=1)
     start = disp[...]
     start_h = halves(start * (1.25 * scale))
     powers = [start] + [stepped(start_h, i) for i in range(BABY - 1)]
-    total = jnp.where(counts == BABY * GIANT, start, 0.0)
-    for j in reversed(range(GIANT)):
+    terms = []
+    for j in range(GIANT):
         term = jnp.zeros((GRAINS, WIDE), F32)
         for i in range(BABY):
             term = jnp.where(counts == BABY * j + i, powers[i], term)
-        total = term + leap(total)
-    part[...] = total
+        terms.append(term)
+    last = jnp.where(counts == BABY * GIANT, start, 0.0)
+    part[...] = terms[0] + leap(0, terms[1] + leap(1, last)) + leap(1, terms[2])
 
     a_row = jnp.broadcast_to(assign[...], (POINTS, POINTS))
     a_col = a_row.T
@@ -171,7 +187,7 @@
     rank = jnp.sum(
         jnp.where((a_row == a_col) & (q_at < p_at), 1.0, 0.0), axis=1, keepdims=True
     ).astype(jnp.int32)
-    column = a_col * 2 + rank
+    column = rank * DEVICES + a_col
     column = jnp.concatenate([column, column], axis=1)
     slot_at = lax.broadcasted_iota(jnp.int32, (POINTS, SLOTS), 1)
     pick = jnp.where(column == slot_at, 1.0, 0.0).astype(BF16)
@@ -189,29 +205,42 @@
     own.wait()
     pltpu.make_async_copy(everything, everything, recv_sem).wait()
 
-    for k in range(CHUNKS):
-        hi, lo = halves(got[pl.ds(k, SLOTS, stride=CHUNKS), :])
-        tile = (dot(pick, hi) + dot(pick, lo)).T
-        first = 128 * k
-        while first < min(128 * k + 128, FLAT):
-            e = first // GRAINS
-            last = min(128 * k + 128, (e + 1) * GRAINS)
-            pos[pl.ds(first - e * GRAINS, last - first), pl.ds(e * POINTS, POINTS)] = tile[
-                first - 128 * k : last - 128 * k
+    def chosen(slots, x):
+        hi, lo = halves(x)
+        return (dot(slots, hi) + dot(slots, lo)).T
+
+    def settle(first, tile):
+        last = first + tile.shape[0]
+        at = first
+        while at < last:
+            e = at // GRAINS
+            end = min(last, (e + 1) * GRAINS)
+            pos[pl.ds(at - e * GRAINS, end - at), pl.ds(e * POINTS, POINTS)] = tile[
+                at - first : end - first
             ]
-            first = last
+            at = end
+
+    for k in range(FULL):
+        both = [got[pl.ds(FULL * c + k, DEVICES, stride=ROWS), :] for c in range(2)]
+        settle(128 * k, chosen(pick, jnp.concatenate(both, axis=0)))
+    tails = got[pl.ds(2 * FULL, DEVICES, stride=ROWS), :]
+    settle(
+        128 * FULL,
+        chosen(pick[:, :DEVICES], tails)[:TAIL] + chosen(pick[:, DEVICES:], tails)[TAIL : 2 * TAIL],
+    )
 
     place = pos[...]
     place_h = halves(place)
     powers = [rate * place] + [stepped(place_h, i) for i in range(BABY - 1)]
     contact = steps_hi[pl.ds(3 * GRAINS, GRAINS), :]
-    pull = scale * place - (dot(contact, place_h[0]) + dot(contact, place_h[1]))
-    total = None
-    for j in reversed(range(GIANT)):
+    pull = scale * place - dot2(contact, place_h)
+    terms = []
+    for j in range(GIANT):
         term = jnp.zeros((GRAINS, WIDE), F32)
         for i in range(BABY):
             term = term + jnp.where(BABY * j + i < counts, powers[i], 0.0)
-        total = term if total is None else term + leap(total)
+        terms.append(term)
+    total = terms[0] + leap(0, terms[1]) + leap(1, terms[2])
 
     def across(x, e):
         return x[:, e * POINTS : (e + 1) * POINTS]
@@ -255,7 +284,7 @@
             device_id_type=MESH,
         )
 
-    for step in range(HELPERS):
+    for step in (4, 5, 3, 2, 6, 7, 1, 0):
         to = lax.rem(helper + step, HELPERS)
         grid_copy(0, 4, 1, high_got, below, to).start()
         grid_copy(12, 4, 2, low_got, above, to).start()
@@ -325,14 +354,15 @@
             pltpu.VMEM((1, POINTS), jnp.int32),
             pltpu.VMEM((CORNERS, POINTS), jnp.int32),
             pltpu.VMEM((3, CORNERS, POINTS), F32),
+            pltpu.VMEM((FULL, SLOTS, 128), F32),
             pltpu.VMEM((DEVICES * ROWS, 128), F32),
             pltpu.VMEM((DEVICES * ROWS, 128), F32),
             pltpu.VMEM((GRAINS, WIDE), F32),
             pltpu.VMEM((GRAINS, WIDE), F32),
             pltpu.VMEM((4 * GRAINS, GRAINS), BF16),
             pltpu.VMEM((3 * GRAINS, GRAINS), BF16),
-            pltpu.VMEM((GRAINS, GRAINS), BF16),
-            pltpu.VMEM((GRAINS, GRAINS), BF16),
+            pltpu.VMEM((2, GRAINS, GRAINS), BF16),
+            pltpu.VMEM((2, GRAINS, GRAINS), BF16),
             pltpu.VMEM((128, CORNERS * POINTS), F32),
             pltpu.VMEM((128, CORNERS * POINTS), BF16),
             pltpu.VMEM((128, 128), F32),
@@ -365,7 +395,8 @@
         in_specs=[vmem] * 3,
         out_specs=(hbm,) * 3,
         scratch_shapes=[pltpu.SemaphoreType.DMA((PIECES + 2,))],
-    )(*outs)
+        compiler_params=pltpu.CompilerParams(vmem_limit_bytes=8 << 20),
+    )(*(pltpu.with_memory_space_constraint(x, pltpu.MemorySpace.VMEM) for x in outs))
     return disp_out.reshape(3, GRAINS, POINTS).transpose(1, 0, 2), stress, grid
 
 

time: 42.7 us -> 37.8 us (0.89)
  Pallas kernels: 39.9 us -> 37 us
  local copies, waits for them, and re-layouts: 2.02 us -> 0 us
    unnamed x6 -> x0, local copies, waits for them, and re-layouts: 2.02 us -> none
    pallas_call x1, Pallas kernels: 38 us -> 36.2 us  [per_device(): pl.pallas_call(kernel, out_shape=tuple((pltpu.VMEM(shape, F32) for shape...]
    pallas_call x1, Pallas kernels: 1.97 us -> 0.89 us  [per_device(): pl.pallas_call(hand_over, out_shape=tuple((jax.ShapeDtypeStruct(shape, F3...]
where the time goes in v3:
time: 37.8 us; the launch traced here: 37.7 us
  Pallas kernels  37 us (98%)
  between operations  0.64 us (2%)
    pallas_call x1, Pallas kernels, per_device(): pl.pallas_call(kernel, out_shape=tuple((pltpu.VMEM(shape, F32) for shape...  36.2 us
    pallas_call x1, Pallas kernels, per_device(): pl.pallas_call(hand_over, out_shape=tuple((jax.ShapeDtypeStruct(shape, F3...  0.89 us

profile of v3, /device:TPU:1, one launch (start us, length us, event | category | flops | bytes accessed | tf_op | source)
XLA Modules:
  0.0 37.7 jit_solution(15177974716011977411)
XLA Ops:
  0.6 36.2 %shard_map.103 = (f32[1200,128]{1,0:T(8,128)S(1)}, f32[9,128]{1,0:T(8,128)S(1)}, f32[3,2,128]{2,1,0:T(2,128)S(1)}) custom-call(f32[1200,256]{1,0:T(8,128)} %bitcast.11, f32[1200,128]{1,0:T(8,128)} %bitcast.12, s32[400,400]{1,0:T(8,128)} %mask_hbm.1, f32[9,128]{1,0:T(8,128)} %strain_hbm.1, s32[1,128]{1,0:T(1,128)} %bitcast.13, s32[1,128]{1,0:T(1,128)} %bitcast.14, ...), custom_call_target="tpu_custom_call" | custom-call | tf_op jit(solution)/shard_map/pallas_call | solution.py:343
  36.8 0.9 %shard_map.104 = (f32[1200,128]{1,0:T(8,128)}, f32[9,128]{1,0:T(8,128)}, f32[3,2,128]{2,1,0:T(2,128)}) custom-call(f32[1200,128]{1,0:T(8,128)S(1)} %get-tuple-element.9.disp_in, f32[9,128]{1,0:T(8,128)S(1)} %get-tuple-element.10.stress_in, f32[3,2,128]{2,1,0:T(2,128)S(1)} %get-tuple-element.11.grid_in), custom_call_target="tpu_custom_call" | custom-call | tf_op jit(solution)/shard_map/pallas_call | solution.py:392

commit v4 on v3

v4 whole, which is shorter than its diff:
```python
import itertools

import jax
import jax.numpy as jnp
from jax import lax
from jax.experimental import pallas as pl
from jax.experimental.pallas import tpu as pltpu
from jax.sharding import PartitionSpec as P

MESH = pl.DeviceIdType.MESH
GRAINS = 400
FLAT = 1200
POINTS = 128
WIDE = 3 * POINTS
SLOTS = 256
HELPERS = 8
SLABS = 16
DEVICES = 128
HEAD = 256
REST = GRAINS - HEAD
TAIL = REST - 128
FIRST = 12
SECOND = 7
CORNERS = 8
BABY = 4
GIANT = 3
F32 = jnp.float32
BF16 = jnp.bfloat16


def halves(x):
    hi = x.astype(BF16)
    lo = (x - hi.astype(F32)).astype(BF16)
    return hi, lo


def dot(a, b):
    return jnp.dot(a, b, preferred_element_type=F32)


def dot2(a, b):
    width = b[0].shape[1]
    both = dot(a, jnp.concatenate(b, axis=1))
    return both[:, :width] + both[:, width:]


def dot3(a, b):
    return dot2(a[0], b) + dot(a[1], b[0])


def dot_nt(a, b):
    return lax.dot_general(a, b, (((1,), (1,)), ((), ())), preferred_element_type=F32)


def ring(a):
    return min(a, 4 - a)


OFFSETS = sorted(
    (
        offset
        for offset in itertools.product(range(4), range(4), range(4), range(2))
        if any(offset)
    ),
    key=lambda o: (-ring(o[0]) - ring(o[1]) - ring(o[2]), (o[0] * 5 + o[1] * 11 + o[2] * 3 + o[3] * 7) % 13),
)


def kernel(
    cached_hbm, disp_hbm, mask_hbm, strain_hbm, counts_hbm, assign_hbm, node_hbm, grads_hbm,
    disp_out, stress_ref, grid_ref,
    cached, disp, mask, strain, counts_ref, assign, node, grads,
    turned, sent_first, sent_second, got_first, got_second, part, pulled, pos, moved,
    steps_hi, steps_lo, contact, hit, spread,
    grid_out, own_got, low_got, high_got,
    load_sem, send_sem, recv_sem, own_sem, grid_own_sem, grid_send, grid_recv,
):
    slab = lax.axis_index("slab")
    helper = lax.axis_index("helper")
    me = slab * HELPERS + helper

    moves = [(cached_hbm, cached)]
    for d in range(3):
        moves.append(
            (disp_hbm.at[pl.ds(d * GRAINS, GRAINS)], disp.at[:, pl.ds(d * POINTS, POINTS)])
        )
    moves += [
        (mask_hbm, mask), (strain_hbm, strain), (counts_hbm, counts_ref),
        (assign_hbm, assign), (node_hbm, node), (grads_hbm, grads),
    ]
    loads = [
        pltpu.make_async_copy(source, target, load_sem.at[i])
        for i, (source, target) in enumerate(moves)
    ]
    for copy in loads:
        copy.start()

    z, x, y, core = slab // 4, lax.rem(slab, 4), helper // 2, lax.rem(helper, 2)
    slab_at = {
        (a, b): lax.rem(z + a, 4) * 4 + lax.rem(x + b, 4) for a in range(4) for b in range(4)
    }
    helper_at = {
        (a, b): lax.rem(y + a, 4) * 2 + lax.rem(core + b, 2) for a in range(4) for b in range(2)
    }
    others = [(slab_at[o[:2]], helper_at[o[2:]]) for o in OFFSETS]

    barrier = pltpu.get_barrier_semaphore()
    for other in others:
        pl.semaphore_signal(barrier, inc=1, device_id=other, device_id_type=MESH)

    @pl.when(slab == 0)
    def _():
        low_got[...] = jnp.zeros_like(low_got)

    @pl.when(slab == SLABS - 1)
    def _():
        high_got[...] = jnp.zeros_like(high_got)

    loads[0].wait()
    for e in range(3):
        for j in range(3):
            turned[3 * e + j] = cached[pl.ds(e * GRAINS + 128 * j, 128), :].T
    tail = [cached[pl.ds(e * GRAINS + GRAINS - TAIL, TAIL), :] for e in range(3)]
    turned[9] = jnp.concatenate(
        tail + tail + [jnp.zeros((128 - 6 * TAIL, SLOTS), F32)], axis=0
    ).T
    for c in range(2):
        mine = pl.ds(c, DEVICES, stride=2)
        for e in range(3):
            for j in range(2):
                sent_first[pl.ds(6 * c + 2 * e + j, DEVICES, stride=FIRST), :] = turned[
                    3 * e + j, mine, :
                ]
            sent_second[pl.ds(3 * c + e, DEVICES, stride=SECOND), :] = turned[3 * e + 2, mine, :]
    lane = lax.broadcasted_iota(jnp.int32, (DEVICES, 128), 1)
    sent_second[pl.ds(6, DEVICES, stride=SECOND), :] = jnp.where(
        lane < 3 * TAIL,
        turned[9, pl.ds(0, DEVICES, stride=2), :],
        turned[9, pl.ds(1, DEVICES, stride=2), :],
    )

    for copy in loads[1:]:
        copy.wait()
    stiff = mask[...].astype(F32)
    scale = jnp.sum(stiff, axis=1, keepdims=True) + 1.0
    rate = 0.8 / scale
    contact[...] = stiff.astype(BF16)

    def prepare():
        rate_row = 0.8 / (jnp.sum(mask[...].astype(F32), axis=0, keepdims=True) + 1.0)
        g_at = lax.broadcasted_iota(jnp.int32, (GRAINS, GRAINS), 0)
        h_at = lax.broadcasted_iota(jnp.int32, (GRAINS, GRAINS), 1)
        once = jnp.where(g_at == h_at, 0.2, 0.0) + rate * mask[...].astype(F32)

        def put(i, power):
            hi, lo = halves(power)
            steps_hi[pl.ds(i * GRAINS, GRAINS), :] = hi
            steps_lo[pl.ds(i * GRAINS, GRAINS), :] = lo
            return hi, lo

        def put_turned(i, power):
            put(i, power * (1.25 * scale) * rate_row)

        put_turned(0, once)
        once_h = halves(once)
        twice = dot3(once_h, once_h)
        put_turned(1, twice)
        twice_h = halves(twice)
        put_turned(2, dot3(twice_h, once_h))
        fourth_h = put(3, dot3(twice_h, twice_h))
        eighth_h = put(4, dot3(fourth_h, fourth_h))
        put(5, dot3(eighth_h, fourth_h))

    pl.semaphore_wait(barrier, DEVICES - 1)

    waves = ((sent_first, got_first, FIRST), (sent_second, got_second, SECOND))
    for wave, (sent, got, rows) in enumerate(waves):
        for to_slab, to_helper in others:
            pltpu.make_async_remote_copy(
                src_ref=sent.at[pl.ds((to_slab * HELPERS + to_helper) * rows, rows)],
                dst_ref=got.at[pl.ds(me * rows, rows)],
                send_sem=send_sem.at[wave],
                recv_sem=recv_sem.at[wave],
                device_id=(to_slab, to_helper),
                device_id_type=MESH,
            ).start()
    own = [
        pltpu.make_async_copy(
            sent.at[pl.ds(me * rows, rows)], got.at[pl.ds(me * rows, rows)], own_sem.at[wave]
        )
        for wave, (sent, got, rows) in enumerate(waves)
    ]
    for copy in own:
        copy.start()

    prepare()

    def step(i):
        rows = pl.ds(i * GRAINS, GRAINS)
        return steps_hi[rows, :], steps_lo[rows, :]

    def leap(i, x):
        return dot3(step(BABY - 2 + i), halves(x))

    counts = jnp.concatenate([counts_ref[...]] * 3, axis=1)
    start = disp[...]
    remainder, quarter = lax.rem(counts, BABY), counts // BABY

    def by(index, choices):
        value = choices[-1]
        for i in reversed(range(len(choices) - 1)):
            value = jnp.where(index == i, choices[i], value)
        return value

    start_h = halves(start * (1.25 * scale))
    moved_start = by(remainder, [start] + [rate * dot3(step(i), start_h) for i in range(BABY - 1)])
    terms = [jnp.where(quarter == j, moved_start, 0.0) for j in range(GIANT + 1)]
    free = terms[0] + leap(1, terms[1]) + leap(2, terms[2]) + leap(3, terms[3])
    part[...] = free
    pulled[...] = scale * free - dot2(contact[...], halves(free))

    a_row = jnp.broadcast_to(assign[...], (POINTS, POINTS))
    a_col = a_row.T
    p_at = lax.broadcasted_iota(jnp.int32, (POINTS, POINTS), 0)
    q_at = lax.broadcasted_iota(jnp.int32, (POINTS, POINTS), 1)
    rank = jnp.sum(
        jnp.where((a_row == a_col) & (q_at < p_at), 1.0, 0.0), axis=1, keepdims=True
    ).astype(jnp.int32)
    column = rank * DEVICES + a_col
    column = jnp.concatenate([column, column], axis=1)
    slot_at = lax.broadcasted_iota(jnp.int32, (POINTS, SLOTS), 1)
    pick = jnp.where(column == slot_at, 1.0, 0.0).astype(BF16)

    for k in range(CORNERS):
        at = node[pl.ds(k, 1), :]
        layer = at // 1024
        target = lax.rem(at, 1024) // 128
        low = lax.rem(at, 128)
        lanes = pl.ds(k * POINTS, POINTS)
        spread[:, lanes] = jnp.where(p_at == low, 1.0, 0.0).astype(BF16)
        hit[:, lanes] = jnp.where(p_at // 4 == target * 4 + layer, 1.0, 0.0)

    def chosen(slots, x):
        hi, lo = halves(x)
        return (dot(slots, hi) + dot(slots, lo)).T

    def arrived(wave):
        own[wave].wait()
        sent, _, rows = waves[wave]
        everything = sent.at[pl.ds(0, (DEVICES - 1) * rows)]
        pltpu.make_async_copy(everything, everything, recv_sem.at[wave]).wait()

    arrived(0)
    for e in range(3):
        for j in range(2):
            both = [
                got_first[pl.ds(6 * c + 2 * e + j, DEVICES, stride=FIRST), :] for c in range(2)
            ]
            pos[pl.ds(128 * j, 128), pl.ds(e * POINTS, POINTS)] = chosen(
                pick, jnp.concatenate(both, axis=0)
            )
    place_h = halves(pos[pl.ds(0, HEAD), :])
    for i in range(2 * BABY - 2):
        hi, lo = step(i)
        moved[pl.ds(i * GRAINS, GRAINS), :] = dot3((hi[:, :HEAD], lo[:, :HEAD]), place_h)

    arrived(1)
    for e in range(3):
        both = [got_second[pl.ds(3 * c + e, DEVICES, stride=SECOND), :] for c in range(2)]
        pos[pl.ds(HEAD, 128), pl.ds(e * POINTS, POINTS)] = chosen(
            pick, jnp.concatenate(both, axis=0)
        )
    tails = got_second[pl.ds(6, DEVICES, stride=SECOND), :]
    tails = (
        chosen(pick[:, :DEVICES], tails)[: 3 * TAIL]
        + chosen(pick[:, DEVICES:], tails)[3 * TAIL : 6 * TAIL]
    )
    for e in range(3):
        pos[pl.ds(HEAD + 128, TAIL), pl.ds(e * POINTS, POINTS)] = tails[e * TAIL : (e + 1) * TAIL]
    place_h = halves(pos[pl.ds(HEAD, REST), :])
    for i in range(2 * BABY - 2):
        hi, lo = step(i)
        rows = pl.ds(i * GRAINS, GRAINS)
        moved[rows, :] = moved[rows, :] + dot3((hi[:, HEAD:], lo[:, HEAD:]), place_h)

    def shifted(i):
        return moved[pl.ds(i * GRAINS, GRAINS), :]

    place = pos[...]
    inner = by(remainder, [place] + [shifted(i) for i in range(BABY - 1)])
    outer = by(quarter, [place] + [shifted(BABY - 1 + i) for i in range(GIANT)])

    def across(x, e):
        return x[:, e * POINTS : (e + 1) * POINTS]

    def over_grains(a, d, b, e):
        return jnp.sum(across(a, d) * across(b, e), axis=0, keepdims=True)

    overlap = [
        [over_grains(place, e, place, f) - over_grains(outer, e, inner, f) for f in range(3)]
        for e in range(3)
    ]
    moments = [
        [
            (
                over_grains(pulled[...], d, place, e)
                + sum(strain[pl.ds(3 * d + f, 1), :] * overlap[e][f] for f in range(3))
            )
            / GRAINS
            for e in range(3)
        ]
        for d in range(3)
    ]
    stress = [[0.5 * (moments[d][e] + moments[e][d]) for e in range(3)] for d in range(3)]
    for d in range(3):
        for e in range(3):
            stress_ref[pl.ds(3 * d + e, 1), :] = stress[d][e]

    nothing = jnp.zeros((1, POINTS), F32)
    rows = [
        jnp.concatenate([stress[0][d], stress[1][d], stress[2][d], nothing] * 2, axis=0)
        for d in range(3)
    ]
    contrib = jnp.concatenate(
        [-sum(rows[d] * grads[d, pl.ds(k, 1), :] for d in range(3)) for k in range(CORNERS)], axis=1
    )
    hi, lo = halves(jnp.concatenate([contrib] * 16, axis=0) * hit[...])
    grid_out[...] = dot_nt(hi, spread[...]) + dot_nt(lo, spread[...])
    def grid_copy(first_row, count, kind, buffer, to_slab, to_helper):
        return pltpu.make_async_remote_copy(
            src_ref=grid_out.at[pl.ds(to_helper * 16 + first_row, count)],
            dst_ref=buffer.at[helper],
            send_sem=grid_send.at[kind],
            recv_sem=grid_recv.at[kind],
            device_id=(to_slab, to_helper),
            device_id_type=MESH,
        )

    order = (4, 5, 3, 2, 6, 7, 1)

    @pl.when(slab > 0)
    def _():
        for ahead in order + (0,):
            grid_copy(0, 4, 1, high_got, slab - 1, lax.rem(helper + ahead, HELPERS)).start()

    for ahead in order:
        grid_copy(4, 8, 0, own_got, slab, lax.rem(helper + ahead, HELPERS)).start()

    @pl.when(slab < SLABS - 1)
    def _():
        for ahead in order + (0,):
            grid_copy(12, 4, 2, low_got, slab + 1, lax.rem(helper + ahead, HELPERS)).start()

    mine = pltpu.make_async_copy(
        grid_out.at[pl.ds(helper * 16 + 4, 8)], own_got.at[helper], grid_own_sem
    )
    mine.start()

    @pl.when(slab >= 0)
    def _():
        place = pos[...]
        powers = [rate * place] + [rate * shifted(i) for i in range(BABY - 1)]
        terms = []
        for j in range(GIANT):
            term = jnp.zeros((GRAINS, WIDE), F32)
            for i in range(BABY):
                term = term + jnp.where(BABY * j + i < counts, powers[i], 0.0)
            terms.append(term)
        total = terms[0] + leap(1, terms[1]) + leap(2, terms[2])
        for d in range(3):
            disp_out[pl.ds(d * GRAINS, GRAINS), :] = part[:, pl.ds(d * POINTS, POINTS)] + sum(
                strain[pl.ds(3 * d + e, 1), :] * across(total, e) for e in range(3)
            )

    mine.wait()

    @pl.when(slab < SLABS - 1)
    def _():
        pltpu.make_async_copy(high_got, high_got, grid_recv.at[1]).wait()

    @pl.when(slab > 0)
    def _():
        pltpu.make_async_copy(low_got, low_got, grid_recv.at[2]).wait()

    seven = own_got.at[pl.ds(0, HELPERS - 1)]
    pltpu.make_async_copy(seven, seven, grid_recv.at[0]).wait()
    here = jnp.sum(own_got[...], axis=0)
    from_below, from_above = jnp.sum(low_got[...], axis=0), jnp.sum(high_got[...], axis=0)
    here = here + jnp.concatenate([from_below, from_above], axis=0)
    for c in range(3):
        for layer in range(2):
            grid_ref[c, pl.ds(layer, 1), :] = here[4 * layer + c : 4 * layer + c + 1]

    for wave, (sent, _, rows) in enumerate(waves):
        everything = sent.at[pl.ds(0, (DEVICES - 1) * rows)]
        pltpu.make_async_copy(everything, everything, send_sem.at[wave]).wait()

    @pl.when(slab > 0)
    def _():
        pltpu.make_async_copy(high_got, high_got, grid_send.at[1]).wait()

    @pl.when(slab < SLABS - 1)
    def _():
        pltpu.make_async_copy(low_got, low_got, grid_send.at[2]).wait()

    pltpu.make_async_copy(seven, seven, grid_send.at[0]).wait()


PIECES = 6


def hand_over(disp_in, stress_in, grid_in, disp_out, stress_out, grid_out, sems):
    rows = FLAT // PIECES
    copies = [
        pltpu.make_async_copy(
            disp_in.at[pl.ds(i * rows, rows)], disp_out.at[pl.ds(i * rows, rows)], sems.at[i]
        )
        for i in range(PIECES)
    ]
    copies.append(pltpu.make_async_copy(stress_in, stress_out, sems.at[PIECES]))
    copies.append(pltpu.make_async_copy(grid_in, grid_out, sems.at[PIECES + 1]))
    for copy in copies:
        copy.start()
    for copy in copies:
        copy.wait()


def per_device(disp, strain, counts, assign, cached_pos, contact_mask, node_index, node_grads):
    vmem = pl.BlockSpec(memory_space=pltpu.VMEM)
    hbm = pl.BlockSpec(memory_space=pltpu.MemorySpace.HBM)
    shapes = ((FLAT, POINTS), (9, POINTS), (3, 2, 128))

    def keep(x):
        return pltpu.with_memory_space_constraint(x, pltpu.MemorySpace.HBM)

    outs = pl.pallas_call(
        kernel,
        out_shape=tuple(pltpu.VMEM(shape, F32) for shape in shapes),
        in_specs=[hbm] * 8,
        out_specs=(vmem,) * 3,
        scratch_shapes=[
            pltpu.VMEM((FLAT, SLOTS), F32),
            pltpu.VMEM((GRAINS, WIDE), F32),
            pltpu.VMEM((GRAINS, GRAINS), jnp.int32),
            pltpu.VMEM((9, POINTS), F32),
            pltpu.VMEM((1, POINTS), jnp.int32),
            pltpu.VMEM((1, POINTS), jnp.int32),
            pltpu.VMEM((CORNERS, POINTS), jnp.int32),
            pltpu.VMEM((3, CORNERS, POINTS), F32),
            pltpu.VMEM((10, SLOTS, 128), F32),
            pltpu.VMEM((DEVICES * FIRST, 128), F32),
            pltpu.VMEM((DEVICES * SECOND, 128), F32),
            pltpu.VMEM((DEVICES * FIRST, 128), F32),
            pltpu.VMEM((DEVICES * SECOND, 128), F32),
            pltpu.VMEM((GRAINS, WIDE), F32),
            pltpu.VMEM((GRAINS, WIDE), F32),
            pltpu.VMEM((GRAINS, WIDE), F32),
            pltpu.VMEM((6 * GRAINS, WIDE), F32),
            pltpu.VMEM((6 * GRAINS, GRAINS), BF16),
            pltpu.VMEM((6 * GRAINS, GRAINS), BF16),
            pltpu.VMEM((GRAINS, GRAINS), BF16),
            pltpu.VMEM((128, CORNERS * POINTS), F32),
            pltpu.VMEM((128, CORNERS * POINTS), BF16),
            pltpu.VMEM((128, 128), F32),
            pltpu.VMEM((HELPERS, 8, 128), F32),
            pltpu.VMEM((HELPERS, 4, 128), F32),
            pltpu.VMEM((HELPERS, 4, 128), F32),
            pltpu.SemaphoreType.DMA((10,)),
            pltpu.SemaphoreType.DMA((2,)),
            pltpu.SemaphoreType.DMA((2,)),
            pltpu.SemaphoreType.DMA((2,)),
            pltpu.SemaphoreType.DMA,
            pltpu.SemaphoreType.DMA((3,)),
            pltpu.SemaphoreType.DMA((3,)),
        ],
        compiler_params=pltpu.CompilerParams(
            collective_id=0, has_side_effects=True, vmem_limit_bytes=56 << 20
        ),
    )(
        keep(cached_pos.transpose(1, 0, 2).reshape(FLAT, SLOTS)),
        keep(disp.transpose(1, 0, 2).reshape(FLAT, POINTS)),
        keep(contact_mask),
        keep(strain),
        keep(counts.reshape(1, POINTS)),
        keep(assign.reshape(1, POINTS)),
        keep(node_index),
        keep(node_grads),
    )
    disp_out, stress, grid = pl.pallas_call(
        hand_over,
        out_shape=tuple(jax.ShapeDtypeStruct(shape, F32) for shape in shapes),
        in_specs=[vmem] * 3,
        out_specs=(hbm,) * 3,
        scratch_shapes=[pltpu.SemaphoreType.DMA((PIECES + 2,))],
        compiler_params=pltpu.CompilerParams(vmem_limit_bytes=8 << 20),
    )(*(pltpu.with_memory_space_constraint(x, pltpu.MemorySpace.VMEM) for x in outs))
    return disp_out.reshape(3, GRAINS, POINTS).transpose(1, 0, 2), stress, grid


def solution(mesh):
    both = ("slab", "helper")
    return jax.shard_map(
        per_device,
        mesh=mesh,
        in_specs=(
            P(None, None, both),
            P(None, both),
            P(both),
            P(both, None),
            P(None, None, both),
            P(),
            P(None, both),
            P(None, None, both),
        ),
        out_specs=(P(None, None, both), P(None, both), P(None, "slab", "helper")),
        check_vma=False,
    )
```

time: 37.8 us -> 35 us (0.926)
  Pallas kernels: 37 us -> 34 us
    pallas_call x1, Pallas kernels: 36.2 us -> 33.1 us  [per_device(): pl.pallas_call(kernel, out_shape=tuple((pltpu.VMEM(shape, F32) for shape...]
where the time goes in v4:
time: 35 us; the launch traced here: 34.8 us
  Pallas kernels  34 us (97%)
  between operations  0.8 us (2%)
    pallas_call x1, Pallas kernels, per_device(): pl.pallas_call(kernel, out_shape=tuple((pltpu.VMEM(shape, F32) for shape...  33.1 us
    pallas_call x1, Pallas kernels, per_device(): pl.pallas_call(hand_over, out_shape=tuple((jax.ShapeDtypeStruct(shape, F3...  0.89 us

profile of v4, /device:TPU:1, one launch (start us, length us, event | category | flops | bytes accessed | tf_op | source)
XLA Modules:
  0.0 34.8 jit_solution(3313618033614427945)
XLA Ops:
  0.6 33.1 %shard_map.103 = (f32[1200,128]{1,0:T(8,128)S(1)}, f32[9,128]{1,0:T(8,128)S(1)}, f32[3,2,128]{2,1,0:T(2,128)S(1)}) custom-call(f32[1200,256]{1,0:T(8,128)} %bitcast.11, f32[1200,128]{1,0:T(8,128)} %bitcast.12, s32[400,400]{1,0:T(8,128)} %mask_hbm.1, f32[9,128]{1,0:T(8,128)} %strain_hbm.1, s32[1,128]{1,0:T(1,128)} %bitcast.13, s32[1,128]{1,0:T(1,128)} %bitcast.14, ...), custom_call_target="tpu_custom_call" | custom-call | tf_op jit(solution)/shard_map/pallas_call | solution.py:436
  33.8 0.9 %shard_map.104 = (f32[1200,128]{1,0:T(8,128)}, f32[9,128]{1,0:T(8,128)}, f32[3,2,128]{2,1,0:T(2,128)}) custom-call(f32[1200,128]{1,0:T(8,128)S(1)} %get-tuple-element.9.disp_in, f32[9,128]{1,0:T(8,128)S(1)} %get-tuple-element.10.stress_in, f32[3,2,128]{2,1,0:T(2,128)S(1)} %get-tuple-element.11.grid_in), custom_call_target="tpu_custom_call" | custom-call | tf_op jit(solution)/shard_map/pallas_call | solution.py:489

commit v5 on v4

--- a/solution.py
+++ b/solution.py
@@ -1,4 +1,5 @@
 import itertools
+import random
 
 import jax
 import jax.numpy as jnp
@@ -56,24 +57,33 @@
     return min(a, 4 - a)
 
 
-OFFSETS = sorted(
-    (
-        offset
-        for offset in itertools.product(range(4), range(4), range(4), range(2))
-        if any(offset)
-    ),
-    key=lambda o: (-ring(o[0]) - ring(o[1]) - ring(o[2]), (o[0] * 5 + o[1] * 11 + o[2] * 3 + o[3] * 7) % 13),
-)
+def hops(offset):
+    return ring(offset[0]) + ring(offset[1]) + ring(offset[2])
+
+
+SHUFFLED = [
+    offset for offset in itertools.product(range(4), range(4), range(4), range(2)) if any(offset)
+]
+random.Random(1).shuffle(SHUFFLED)
+FARTHEST = sorted(SHUFFLED, key=lambda offset: -hops(offset))
+
+
+def in_plane(offset):
+    return 0 in offset[:3]
+
+
+NEAR = [offset for offset in FARTHEST if in_plane(offset)]
+ORDERS = (sorted(SHUFFLED, key=lambda offset: not in_plane(offset)), FARTHEST)
 
 
 def kernel(
     cached_hbm, disp_hbm, mask_hbm, strain_hbm, counts_hbm, assign_hbm, node_hbm, grads_hbm,
     disp_out, stress_ref, grid_ref,
     cached, disp, mask, strain, counts_ref, assign, node, grads,
-    turned, sent_first, sent_second, got_first, got_second, part, pulled, pos, moved,
-    steps_hi, steps_lo, contact, hit, spread,
+    turned, sent_first, sent_second, got_first, got_second, part, pulled, pos, met,
+    steps_hi, steps_lo, first_hi, first_lo, second_hi, second_lo, contact, hit, spread,
     grid_out, own_got, low_got, high_got,
-    load_sem, send_sem, recv_sem, own_sem, grid_own_sem, grid_send, grid_recv,
+    load_sem, line_sem, send_sem, recv_sem, own_sem, grid_own_sem, grid_send, grid_recv,
 ):
     slab = lax.axis_index("slab")
     helper = lax.axis_index("helper")
@@ -102,11 +112,13 @@
     helper_at = {
         (a, b): lax.rem(y + a, 4) * 2 + lax.rem(core + b, 2) for a in range(4) for b in range(2)
     }
-    others = [(slab_at[o[:2]], helper_at[o[2:]]) for o in OFFSETS]
+
+    def at(offset):
+        return slab_at[offset[:2]], helper_at[offset[2:]]
 
     barrier = pltpu.get_barrier_semaphore()
-    for other in others:
-        pl.semaphore_signal(barrier, inc=1, device_id=other, device_id_type=MESH)
+    for offset in NEAR:
+        pl.semaphore_signal(barrier, inc=1, device_id=at(offset), device_id_type=MESH)
 
     @pl.when(slab == 0)
     def _():
@@ -156,6 +168,11 @@
             hi, lo = halves(power)
             steps_hi[pl.ds(i * GRAINS, GRAINS), :] = hi
             steps_lo[pl.ds(i * GRAINS, GRAINS), :] = lo
+            side, at = i // GIANT, i % GIANT
+            first_hi[side, :, pl.ds(at * HEAD, HEAD)] = hi[:, :HEAD]
+            first_lo[side, :, pl.ds(at * HEAD, HEAD)] = lo[:, :HEAD]
+            second_hi[side, :, pl.ds(at * REST, REST)] = hi[:, HEAD:]
+            second_lo[side, :, pl.ds(at * REST, REST)] = lo[:, HEAD:]
             return hi, lo
 
         def put_turned(i, power):
@@ -171,11 +188,16 @@
         eighth_h = put(4, dot3(fourth_h, fourth_h))
         put(5, dot3(eighth_h, fourth_h))
 
-    pl.semaphore_wait(barrier, DEVICES - 1)
+    pl.semaphore_wait(barrier, len(NEAR))
+    for a in (2, 1, 3):
+        pl.semaphore_signal(line_sem, inc=1, device_id=at((a, 0, 0, 0)), device_id_type=MESH)
 
     waves = ((sent_first, got_first, FIRST), (sent_second, got_second, SECOND))
     for wave, (sent, got, rows) in enumerate(waves):
-        for to_slab, to_helper in others:
+        for i, offset in enumerate(ORDERS[wave]):
+            if wave == 0 and i == len(NEAR):
+                pl.semaphore_wait(line_sem, 3)
+            to_slab, to_helper = at(offset)
             pltpu.make_async_remote_copy(
                 src_ref=sent.at[pl.ds((to_slab * HELPERS + to_helper) * rows, rows)],
                 dst_ref=got.at[pl.ds(me * rows, rows)],
@@ -232,10 +254,10 @@
     pick = jnp.where(column == slot_at, 1.0, 0.0).astype(BF16)
 
     for k in range(CORNERS):
-        at = node[pl.ds(k, 1), :]
-        layer = at // 1024
-        target = lax.rem(at, 1024) // 128
-        low = lax.rem(at, 128)
+        value = node[pl.ds(k, 1), :]
+        layer = value // 1024
+        target = lax.rem(value, 1024) // 128
+        low = lax.rem(value, 128)
         lanes = pl.ds(k * POINTS, POINTS)
         spread[:, lanes] = jnp.where(p_at == low, 1.0, 0.0).astype(BF16)
         hit[:, lanes] = jnp.where(p_at // 4 == target * 4 + layer, 1.0, 0.0)
@@ -249,6 +271,10 @@
         sent, _, rows = waves[wave]
         everything = sent.at[pl.ds(0, (DEVICES - 1) * rows)]
         pltpu.make_async_copy(everything, everything, recv_sem.at[wave]).wait()
+
+    def masked(index, x_h):
+        keeps = [jnp.where(index == i + 1, 1.0, 0.0).astype(BF16) for i in range(GIANT)]
+        return [jnp.concatenate([x * keep for keep in keeps], axis=0) for x in x_h]
 
     arrived(0)
     for e in range(3):
@@ -260,9 +286,9 @@
                 pick, jnp.concatenate(both, axis=0)
             )
     place_h = halves(pos[pl.ds(0, HEAD), :])
-    for i in range(2 * BABY - 2):
-        hi, lo = step(i)
-        moved[pl.ds(i * GRAINS, GRAINS), :] = dot3((hi[:, :HEAD], lo[:, :HEAD]), place_h)
+    sides = (remainder, quarter)
+    for side, index in enumerate(sides):
+        met[side] = dot3((first_hi[side], first_lo[side]), masked(index, place_h))
 
     arrived(1)
     for e in range(3):
@@ -278,17 +304,12 @@
     for e in range(3):
         pos[pl.ds(HEAD + 128, TAIL), pl.ds(e * POINTS, POINTS)] = tails[e * TAIL : (e + 1) * TAIL]
     place_h = halves(pos[pl.ds(HEAD, REST), :])
-    for i in range(2 * BABY - 2):
-        hi, lo = step(i)
-        rows = pl.ds(i * GRAINS, GRAINS)
-        moved[rows, :] = moved[rows, :] + dot3((hi[:, HEAD:], lo[:, HEAD:]), place_h)
-
-    def shifted(i):
-        return moved[pl.ds(i * GRAINS, GRAINS), :]
-
     place = pos[...]
-    inner = by(remainder, [place] + [shifted(i) for i in range(BABY - 1)])
-    outer = by(quarter, [place] + [shifted(BABY - 1 + i) for i in range(GIANT)])
+    inner, outer = [
+        jnp.where(index == 0, place, met[side])
+        + dot3((second_hi[side], second_lo[side]), masked(index, place_h))
+        for side, index in enumerate(sides)
+    ]
 
     def across(x, e):
         return x[:, e * POINTS : (e + 1) * POINTS]
@@ -359,7 +380,8 @@
     @pl.when(slab >= 0)
     def _():
         place = pos[...]
-        powers = [rate * place] + [rate * shifted(i) for i in range(BABY - 1)]
+        place_h = halves(place)
+        powers = [rate * place] + [rate * dot3(step(i), place_h) for i in range(BABY - 1)]
         terms = []
         for j in range(GIANT):
             term = jnp.zeros((GRAINS, WIDE), F32)
@@ -455,9 +477,13 @@
             pltpu.VMEM((GRAINS, WIDE), F32),
             pltpu.VMEM((GRAINS, WIDE), F32),
             pltpu.VMEM((GRAINS, WIDE), F32),
-            pltpu.VMEM((6 * GRAINS, WIDE), F32),
+            pltpu.VMEM((2, GRAINS, WIDE), F32),
             pltpu.VMEM((6 * GRAINS, GRAINS), BF16),
             pltpu.VMEM((6 * GRAINS, GRAINS), BF16),
+            pltpu.VMEM((2, GRAINS, GIANT * HEAD), BF16),
+            pltpu.VMEM((2, GRAINS, GIANT * HEAD), BF16),
+            pltpu.VMEM((2, GRAINS, GIANT * REST), BF16),
+            pltpu.VMEM((2, GRAINS, GIANT * REST), BF16),
             pltpu.VMEM((GRAINS, GRAINS), BF16),
             pltpu.VMEM((128, CORNERS * POINTS), F32),
             pltpu.VMEM((128, CORNERS * POINTS), BF16),
@@ -466,6 +492,7 @@
             pltpu.VMEM((HELPERS, 4, 128), F32),
             pltpu.VMEM((HELPERS, 4, 128), F32),
             pltpu.SemaphoreType.DMA((10,)),
+            pltpu.SemaphoreType.REGULAR,
             pltpu.SemaphoreType.DMA((2,)),
             pltpu.SemaphoreType.DMA((2,)),
             pltpu.SemaphoreType.DMA((2,)),

time: 35 us -> 33.4 us (0.954)
  Pallas kernels: 34 us -> 32.5 us
    pallas_call x1, Pallas kernels: 33.1 us -> 31.6 us  [per_device(): pl.pallas_call(kernel, out_shape=tuple((pltpu.VMEM(shape, F32) for shape...]
where the time goes in v5:
time: 33.4 us; the launch traced here: 33.3 us
  Pallas kernels  32.5 us (97%)
  between operations  0.8 us (2%)
    pallas_call x1, Pallas kernels, per_device(): pl.pallas_call(kernel, out_shape=tuple((pltpu.VMEM(shape, F32) for shape...  31.6 us
    pallas_call x1, Pallas kernels, per_device(): pl.pallas_call(hand_over, out_shape=tuple((jax.ShapeDtypeStruct(shape, F3...  0.89 us

profile of v5, /device:TPU:1, one launch (start us, length us, event | category | flops | bytes accessed | tf_op | source)
XLA Modules:
  0.0 33.3 jit_solution(11902333961137584984)
XLA Ops:
  0.6 31.6 %shard_map.103 = (f32[1200,128]{1,0:T(8,128)S(1)}, f32[9,128]{1,0:T(8,128)S(1)}, f32[3,2,128]{2,1,0:T(2,128)S(1)}) custom-call(f32[1200,256]{1,0:T(8,128)} %bitcast.11, f32[1200,128]{1,0:T(8,128)} %bitcast.12, s32[400,400]{1,0:T(8,128)} %mask_hbm.1, f32[9,128]{1,0:T(8,128)} %strain_hbm.1, s32[1,128]{1,0:T(1,128)} %bitcast.13, s32[1,128]{1,0:T(1,128)} %bitcast.14, ...), custom_call_target="tpu_custom_call" | custom-call | tf_op jit(solution)/shard_map/pallas_call | solution.py:458
  32.2 0.9 %shard_map.104 = (f32[1200,128]{1,0:T(8,128)}, f32[9,128]{1,0:T(8,128)}, f32[3,2,128]{2,1,0:T(2,128)}) custom-call(f32[1200,128]{1,0:T(8,128)S(1)} %get-tuple-element.9.disp_in, f32[9,128]{1,0:T(8,128)S(1)} %get-tuple-element.10.stress_in, f32[3,2,128]{2,1,0:T(2,128)S(1)} %get-tuple-element.11.grid_in), custom_call_target="tpu_custom_call" | custom-call | tf_op jit(solution)/shard_map/pallas_call | solution.py:516

commit v6 on v5

--- a/solution.py
+++ b/solution.py
@@ -228,16 +228,23 @@
     start = disp[...]
     remainder, quarter = lax.rem(counts, BABY), counts // BABY
 
-    def by(index, choices):
-        value = choices[-1]
-        for i in reversed(range(len(choices) - 1)):
-            value = jnp.where(index == i, choices[i], value)
-        return value
-
-    start_h = halves(start * (1.25 * scale))
-    moved_start = by(remainder, [start] + [rate * dot3(step(i), start_h) for i in range(BABY - 1)])
-    terms = [jnp.where(quarter == j, moved_start, 0.0) for j in range(GIANT + 1)]
-    free = terms[0] + leap(1, terms[1]) + leap(2, terms[2]) + leap(3, terms[3])
+    sides = (remainder, quarter)
+
+    def masked(index, x_h):
+        keeps = [jnp.where(index == i + 1, 1.0, 0.0).astype(BF16) for i in range(GIANT)]
+        return [jnp.concatenate([x * keep for keep in keeps], axis=0) for x in x_h]
+
+    def first_part(side, x_h):
+        return dot3((first_hi[side], first_lo[side]), masked(sides[side], x_h))
+
+    def second_part(side, x_h):
+        return dot3((second_hi[side], second_lo[side]), masked(sides[side], x_h))
+
+    def whole(side, x):
+        return first_part(side, halves(x[:HEAD])) + second_part(side, halves(x[HEAD:]))
+
+    free = jnp.where(remainder == 0, start, rate * whole(0, start * (1.25 * scale)))
+    free = jnp.where(quarter == 0, free, whole(1, free))
     part[...] = free
     pulled[...] = scale * free - dot2(contact[...], halves(free))
 
@@ -272,10 +279,6 @@
         everything = sent.at[pl.ds(0, (DEVICES - 1) * rows)]
         pltpu.make_async_copy(everything, everything, recv_sem.at[wave]).wait()
 
-    def masked(index, x_h):
-        keeps = [jnp.where(index == i + 1, 1.0, 0.0).astype(BF16) for i in range(GIANT)]
-        return [jnp.concatenate([x * keep for keep in keeps], axis=0) for x in x_h]
-
     arrived(0)
     for e in range(3):
         for j in range(2):
@@ -286,9 +289,8 @@
                 pick, jnp.concatenate(both, axis=0)
             )
     place_h = halves(pos[pl.ds(0, HEAD), :])
-    sides = (remainder, quarter)
-    for side, index in enumerate(sides):
-        met[side] = dot3((first_hi[side], first_lo[side]), masked(index, place_h))
+    for side in range(2):
+        met[side] = first_part(side, place_h)
 
     arrived(1)
     for e in range(3):
@@ -306,8 +308,7 @@
     place_h = halves(pos[pl.ds(HEAD, REST), :])
     place = pos[...]
     inner, outer = [
-        jnp.where(index == 0, place, met[side])
-        + dot3((second_hi[side], second_lo[side]), masked(index, place_h))
+        jnp.where(index == 0, place, met[side]) + second_part(side, place_h)
         for side, index in enumerate(sides)
     ]
 

time: 33.4 us -> 33.4 us (level)
  no operation moved by 1% of the time
where the time goes in v6:
time: 33.4 us; the launch traced here: 33.3 us
  Pallas kernels  32.5 us (97%)
  between operations  0.8 us (2%)
    pallas_call x1, Pallas kernels, per_device(): pl.pallas_call(kernel, out_shape=tuple((pltpu.VMEM(shape, F32) for shape...  31.6 us
    pallas_call x1, Pallas kernels, per_device(): pl.pallas_call(hand_over, out_shape=tuple((jax.ShapeDtypeStruct(shape, F3...  0.89 us

profile of v6, /device:TPU:1, one launch (start us, length us, event | category | flops | bytes accessed | tf_op | source)
XLA Modules:
  0.0 33.3 jit_solution(6743816330972596210)
XLA Ops:
  0.6 31.6 %shard_map.103 = (f32[1200,128]{1,0:T(8,128)S(1)}, f32[9,128]{1,0:T(8,128)S(1)}, f32[3,2,128]{2,1,0:T(2,128)S(1)}) custom-call(f32[1200,256]{1,0:T(8,128)} %bitcast.11, f32[1200,128]{1,0:T(8,128)} %bitcast.12, s32[400,400]{1,0:T(8,128)} %mask_hbm.1, f32[9,128]{1,0:T(8,128)} %strain_hbm.1, s32[1,128]{1,0:T(1,128)} %bitcast.13, s32[1,128]{1,0:T(1,128)} %bitcast.14, ...), custom_call_target="tpu_custom_call" | custom-call | tf_op jit(solution)/shard_map/pallas_call | solution.py:459
  32.2 0.9 %shard_map.104 = (f32[1200,128]{1,0:T(8,128)}, f32[9,128]{1,0:T(8,128)}, f32[3,2,128]{2,1,0:T(2,128)}) custom-call(f32[1200,128]{1,0:T(8,128)S(1)} %get-tuple-element.9.disp_in, f32[9,128]{1,0:T(8,128)S(1)} %get-tuple-element.10.stress_in, f32[3,2,128]{2,1,0:T(2,128)S(1)} %get-tuple-element.11.grid_in), custom_call_target="tpu_custom_call" | custom-call | tf_op jit(solution)/shard_map/pallas_call | solution.py:517

commit v7 on v6

--- a/solution.py
+++ b/solution.py
@@ -45,6 +45,14 @@
     return both[:, :width] + both[:, width:]
 
 
+def dot_exact(a, x):
+    hi = x.astype(BF16)
+    mid, lo = halves(x - hi.astype(F32))
+    width = x.shape[1]
+    both = dot(a, jnp.concatenate([hi, mid, lo], axis=1))
+    return both[:, :width] + (both[:, width : 2 * width] + both[:, 2 * width :])
+
+
 def dot3(a, b):
     return dot2(a[0], b) + dot(a[1], b[0])
 
@@ -81,7 +89,7 @@
     disp_out, stress_ref, grid_ref,
     cached, disp, mask, strain, counts_ref, assign, node, grads,
     turned, sent_first, sent_second, got_first, got_second, part, pulled, pos, met,
-    steps_hi, steps_lo, first_hi, first_lo, second_hi, second_lo, contact, hit, spread,
+    sums_hi, sums_lo, leaps_hi, leaps_lo, first_hi, first_lo, second_hi, second_lo, contact, hit, spread,
     grid_out, own_got, low_got, high_got,
     load_sem, line_sem, send_sem, recv_sem, own_sem, grid_own_sem, grid_send, grid_recv,
 ):
@@ -129,64 +137,30 @@
         high_got[...] = jnp.zeros_like(high_got)
 
     loads[0].wait()
+    def slot(c):
+        return pl.ds(c, DEVICES, stride=2)
+
     for e in range(3):
-        for j in range(3):
-            turned[3 * e + j] = cached[pl.ds(e * GRAINS + 128 * j, 128), :].T
-    tail = [cached[pl.ds(e * GRAINS + GRAINS - TAIL, TAIL), :] for e in range(3)]
-    turned[9] = jnp.concatenate(
-        tail + tail + [jnp.zeros((128 - 6 * TAIL, SLOTS), F32)], axis=0
-    ).T
-    for c in range(2):
-        mine = pl.ds(c, DEVICES, stride=2)
+        for j in range(2):
+            turned[2 * e + j] = cached[pl.ds(e * GRAINS + 128 * j, 128), :].T
+            for c in range(2):
+                sent_first[pl.ds(6 * c + 2 * e + j, DEVICES, stride=FIRST), :] = turned[
+                    2 * e + j, slot(c), :
+                ]
+
+    def fill_second():
         for e in range(3):
-            for j in range(2):
-                sent_first[pl.ds(6 * c + 2 * e + j, DEVICES, stride=FIRST), :] = turned[
-                    3 * e + j, mine, :
-                ]
-            sent_second[pl.ds(3 * c + e, DEVICES, stride=SECOND), :] = turned[3 * e + 2, mine, :]
-    lane = lax.broadcasted_iota(jnp.int32, (DEVICES, 128), 1)
-    sent_second[pl.ds(6, DEVICES, stride=SECOND), :] = jnp.where(
-        lane < 3 * TAIL,
-        turned[9, pl.ds(0, DEVICES, stride=2), :],
-        turned[9, pl.ds(1, DEVICES, stride=2), :],
-    )
-
-    for copy in loads[1:]:
-        copy.wait()
-    stiff = mask[...].astype(F32)
-    scale = jnp.sum(stiff, axis=1, keepdims=True) + 1.0
-    rate = 0.8 / scale
-    contact[...] = stiff.astype(BF16)
-
-    def prepare():
-        rate_row = 0.8 / (jnp.sum(mask[...].astype(F32), axis=0, keepdims=True) + 1.0)
-        g_at = lax.broadcasted_iota(jnp.int32, (GRAINS, GRAINS), 0)
-        h_at = lax.broadcasted_iota(jnp.int32, (GRAINS, GRAINS), 1)
-        once = jnp.where(g_at == h_at, 0.2, 0.0) + rate * mask[...].astype(F32)
-
-        def put(i, power):
-            hi, lo = halves(power)
-            steps_hi[pl.ds(i * GRAINS, GRAINS), :] = hi
-            steps_lo[pl.ds(i * GRAINS, GRAINS), :] = lo
-            side, at = i // GIANT, i % GIANT
-            first_hi[side, :, pl.ds(at * HEAD, HEAD)] = hi[:, :HEAD]
-            first_lo[side, :, pl.ds(at * HEAD, HEAD)] = lo[:, :HEAD]
-            second_hi[side, :, pl.ds(at * REST, REST)] = hi[:, HEAD:]
-            second_lo[side, :, pl.ds(at * REST, REST)] = lo[:, HEAD:]
-            return hi, lo
-
-        def put_turned(i, power):
-            put(i, power * (1.25 * scale) * rate_row)
-
-        put_turned(0, once)
-        once_h = halves(once)
-        twice = dot3(once_h, once_h)
-        put_turned(1, twice)
-        twice_h = halves(twice)
-        put_turned(2, dot3(twice_h, once_h))
-        fourth_h = put(3, dot3(twice_h, twice_h))
-        eighth_h = put(4, dot3(fourth_h, fourth_h))
-        put(5, dot3(eighth_h, fourth_h))
+            turned[6 + e] = cached[pl.ds(e * GRAINS + HEAD, 128), :].T
+            for c in range(2):
+                sent_second[pl.ds(3 * c + e, DEVICES, stride=SECOND), :] = turned[6 + e, slot(c), :]
+        tail = [cached[pl.ds(e * GRAINS + GRAINS - TAIL, TAIL), :] for e in range(3)]
+        turned[9] = jnp.concatenate(
+            tail + tail + [jnp.zeros((128 - 6 * TAIL, SLOTS), F32)], axis=0
+        ).T
+        lane = lax.broadcasted_iota(jnp.int32, (DEVICES, 128), 1)
+        sent_second[pl.ds(6, DEVICES, stride=SECOND), :] = jnp.where(
+            lane < 3 * TAIL, turned[9, slot(0), :], turned[9, slot(1), :]
+        )
 
     pl.semaphore_wait(barrier, len(NEAR))
     for a in (2, 1, 3):
@@ -194,6 +168,8 @@
 
     waves = ((sent_first, got_first, FIRST), (sent_second, got_second, SECOND))
     for wave, (sent, got, rows) in enumerate(waves):
+        if wave == 1:
+            fill_second()
         for i, offset in enumerate(ORDERS[wave]):
             if wave == 0 and i == len(NEAR):
                 pl.semaphore_wait(line_sem, 3)
@@ -215,14 +191,59 @@
     for copy in own:
         copy.start()
 
+    for copy in loads[1:]:
+        copy.wait()
+    stiff = mask[...].astype(F32)
+    scale = jnp.sum(stiff, axis=1, keepdims=True) + 1.0
+    rate = 0.8 / scale
+    contact[...] = stiff.astype(BF16)
+
+    def prepare():
+        rate_row = 0.8 / (jnp.sum(mask[...].astype(F32), axis=0, keepdims=True) + 1.0)
+        g_at = lax.broadcasted_iota(jnp.int32, (GRAINS, GRAINS), 0)
+        h_at = lax.broadcasted_iota(jnp.int32, (GRAINS, GRAINS), 1)
+        once = jnp.where(g_at == h_at, 0.2, 0.0) + rate * mask[...].astype(F32)
+
+        def put(i, power):
+            hi, lo = halves(power)
+            side, at = i // GIANT, i % GIANT
+            first_hi[side, :, pl.ds(at * HEAD, HEAD)] = hi[:, :HEAD]
+            first_lo[side, :, pl.ds(at * HEAD, HEAD)] = lo[:, :HEAD]
+            second_hi[side, :, pl.ds(at * REST, REST)] = hi[:, HEAD:]
+            second_lo[side, :, pl.ds(at * REST, REST)] = lo[:, HEAD:]
+            return hi, lo
+
+        def put_turned(i, power):
+            put(i, power * (1.25 * scale) * rate_row)
+
+        def put_sum(i, value):
+            sums_hi[i], sums_lo[i] = halves(value)
+
+        put_turned(0, once)
+        once_h = halves(once)
+        summed = (jnp.where(g_at == h_at, 1.0, 0.0) + once) * rate_row
+        put_sum(0, summed)
+        twice = dot3(once_h, once_h)
+        put_turned(1, twice)
+        summed = summed + twice * rate_row
+        put_sum(1, summed)
+        twice_h = halves(twice)
+        thrice = dot3(twice_h, once_h)
+        put_turned(2, thrice)
+        put_sum(2, summed + thrice * rate_row)
+        fourth_h = put(3, dot3(twice_h, twice_h))
+        leaps_hi[0], leaps_lo[0] = fourth_h
+        eighth_h = put(4, dot3(fourth_h, fourth_h))
+        leaps_hi[1], leaps_lo[1] = eighth_h
+        put(5, dot3(eighth_h, fourth_h))
+
     prepare()
 
-    def step(i):
-        rows = pl.ds(i * GRAINS, GRAINS)
-        return steps_hi[rows, :], steps_lo[rows, :]
+    def summed(i, x_h):
+        return dot3((sums_hi[i], sums_lo[i]), x_h)
 
     def leap(i, x):
-        return dot3(step(BABY - 2 + i), halves(x))
+        return dot3((leaps_hi[i], leaps_lo[i]), halves(x))
 
     counts = jnp.concatenate([counts_ref[...]] * 3, axis=1)
     start = disp[...]
@@ -246,7 +267,7 @@
     free = jnp.where(remainder == 0, start, rate * whole(0, start * (1.25 * scale)))
     free = jnp.where(quarter == 0, free, whole(1, free))
     part[...] = free
-    pulled[...] = scale * free - dot2(contact[...], halves(free))
+    pulled[...] = scale * free - dot_exact(contact[...], free)
 
     a_row = jnp.broadcast_to(assign[...], (POINTS, POINTS))
     a_col = a_row.T
@@ -382,14 +403,20 @@
     def _():
         place = pos[...]
         place_h = halves(place)
-        powers = [rate * place] + [rate * dot3(step(i), place_h) for i in range(BABY - 1)]
-        terms = []
-        for j in range(GIANT):
-            term = jnp.zeros((GRAINS, WIDE), F32)
-            for i in range(BABY):
-                term = term + jnp.where(BABY * j + i < counts, powers[i], 0.0)
-            terms.append(term)
-        total = terms[0] + leap(1, terms[1]) + leap(2, terms[2])
+
+        def only(index):
+            keep = jnp.where(remainder == index, 1.0, 0.0).astype(BF16)
+            return [x * keep for x in place_h]
+
+        some = (
+            jnp.where(remainder == 1, rate * place, 0.0) + summed(0, only(2)) + summed(1, only(3))
+        )
+        full = summed(2, place_h)
+
+        def term(j):
+            return jnp.where(quarter > j, full, jnp.where(quarter == j, some, 0.0))
+
+        total = term(0) + leap(0, term(1)) + leap(1, term(2))
         for d in range(3):
             disp_out[pl.ds(d * GRAINS, GRAINS), :] = part[:, pl.ds(d * POINTS, POINTS)] + sum(
                 strain[pl.ds(3 * d + e, 1), :] * across(total, e) for e in range(3)
@@ -479,8 +506,10 @@
             pltpu.VMEM((GRAINS, WIDE), F32),
             pltpu.VMEM((GRAINS, WIDE), F32),
             pltpu.VMEM((2, GRAINS, WIDE), F32),
-            pltpu.VMEM((6 * GRAINS, GRAINS), BF16),
-            pltpu.VMEM((6 * GRAINS, GRAINS), BF16),
+            pltpu.VMEM((GIANT, GRAINS, GRAINS), BF16),
+            pltpu.VMEM((GIANT, GRAINS, GRAINS), BF16),
+            pltpu.VMEM((2, GRAINS, GRAINS), BF16),
+            pltpu.VMEM((2, GRAINS, GRAINS), BF16),
             pltpu.VMEM((2, GRAINS, GIANT * HEAD), BF16),
             pltpu.VMEM((2, GRAINS, GIANT * HEAD), BF16),
             pltpu.VMEM((2, GRAINS, GIANT * REST), BF16),

time: 33.4 us -> 33.5 us (level)
  no operation moved by 1% of the time
where the time goes in v7:
time: 33.5 us; the launch traced here: 33.3 us
  Pallas kernels  32.5 us (97%)
  between operations  0.82 us (2%)
    pallas_call x1, Pallas kernels, per_device(): pl.pallas_call(kernel, out_shape=tuple((pltpu.VMEM(shape, F32) for shape...  31.6 us
    pallas_call x1, Pallas kernels, per_device(): pl.pallas_call(hand_over, out_shape=tuple((jax.ShapeDtypeStruct(shape, F3...  0.89 us

profile of v7, /device:TPU:1, one launch (start us, length us, event | category | flops | bytes accessed | tf_op | source)
XLA Modules:
  0.0 33.3 jit_solution(11646210416792548125)
XLA Ops:
  0.6 31.6 %shard_map.103 = (f32[1200,128]{1,0:T(8,128)S(1)}, f32[9,128]{1,0:T(8,128)S(1)}, f32[3,2,128]{2,1,0:T(2,128)S(1)}) custom-call(f32[1200,256]{1,0:T(8,128)} %bitcast.11, f32[1200,128]{1,0:T(8,128)} %bitcast.12, s32[400,400]{1,0:T(8,128)} %mask_hbm.1, f32[9,128]{1,0:T(8,128)} %strain_hbm.1, s32[1,128]{1,0:T(1,128)} %bitcast.13, s32[1,128]{1,0:T(1,128)} %bitcast.14, ...), custom_call_target="tpu_custom_call" | custom-call | tf_op jit(solution)/shard_map/pallas_call | solution.py:486
  32.3 0.9 %shard_map.104 = (f32[1200,128]{1,0:T(8,128)}, f32[9,128]{1,0:T(8,128)}, f32[3,2,128]{2,1,0:T(2,128)}) custom-call(f32[1200,128]{1,0:T(8,128)S(1)} %get-tuple-element.9.disp_in, f32[9,128]{1,0:T(8,128)S(1)} %get-tuple-element.10.stress_in, f32[3,2,128]{2,1,0:T(2,128)S(1)} %get-tuple-element.11.grid_in), custom_call_target="tpu_custom_call" | custom-call | tf_op jit(solution)/shard_map/pallas_call | solution.py:546

commit v8 on v5

--- a/solution.py
+++ b/solution.py
@@ -73,7 +73,7 @@
 
 
 NEAR = [offset for offset in FARTHEST if in_plane(offset)]
-ORDERS = (sorted(SHUFFLED, key=lambda offset: not in_plane(offset)), FARTHEST)
+ORDERS = (sorted(FARTHEST, key=lambda offset: not in_plane(offset)), FARTHEST)
 
 
 def kernel(

time: 33.4 us -> 33.4 us (level)
  no operation moved by 1% of the time
where the time goes in v8:
time: 33.4 us; the launch traced here: 33.3 us
  Pallas kernels  32.5 us (97%)
  between operations  0.8 us (2%)
    pallas_call x1, Pallas kernels, per_device(): pl.pallas_call(kernel, out_shape=tuple((pltpu.VMEM(shape, F32) for shape...  31.6 us
    pallas_call x1, Pallas kernels, per_device(): pl.pallas_call(hand_over, out_shape=tuple((jax.ShapeDtypeStruct(shape, F3...  0.89 us

profile of v8, /device:TPU:1, one launch (start us, length us, event | category | flops | bytes accessed | tf_op | source)
XLA Modules:
  0.0 33.3 jit_solution(14495205449987208878)
XLA Ops:
  0.6 31.6 %shard_map.103 = (f32[1200,128]{1,0:T(8,128)S(1)}, f32[9,128]{1,0:T(8,128)S(1)}, f32[3,2,128]{2,1,0:T(2,128)S(1)}) custom-call(f32[1200,256]{1,0:T(8,128)} %bitcast.11, f32[1200,128]{1,0:T(8,128)} %bitcast.12, s32[400,400]{1,0:T(8,128)} %mask_hbm.1, f32[9,128]{1,0:T(8,128)} %strain_hbm.1, s32[1,128]{1,0:T(1,128)} %bitcast.13, s32[1,128]{1,0:T(1,128)} %bitcast.14, ...), custom_call_target="tpu_custom_call" | custom-call | tf_op jit(solution)/shard_map/pallas_call | solution.py:458
  32.2 0.9 %shard_map.104 = (f32[1200,128]{1,0:T(8,128)}, f32[9,128]{1,0:T(8,128)}, f32[3,2,128]{2,1,0:T(2,128)}) custom-call(f32[1200,128]{1,0:T(8,128)S(1)} %get-tuple-element.9.disp_in, f32[9,128]{1,0:T(8,128)S(1)} %get-tuple-element.10.stress_in, f32[3,2,128]{2,1,0:T(2,128)S(1)} %get-tuple-element.11.grid_in), custom_call_target="tpu_custom_call" | custom-call | tf_op jit(solution)/shard_map/pallas_call | solution.py:516
